TPU v7x, 32 devices: a whole 2x2x4 slice. The times are simulated.
32 devices in a mesh: space: 8 (over z, x), tm: 4 (over y, core).
Axes of the slice: x: 2, y: 2, z: 4, core: 2. Of those that a mesh axis runs over, the one named last changes fastest.
Arguments:
- eigvecs: float32 [4, 2, 3, 64, 8, 144], P('tm', None, None, None, 'space'), may hold values from -6 to 6
- gauge_links: float32 [3, 4, 2, 3, 3, 8, 144], P(None, 'tm', None, None, None, 'space'), may hold values from -4 to 4
- perambulators: bfloat16 [4, 4, 2, 4, 4, 64, 64], P('tm'), may hold values from -0.375 to 0.375
- momenta: int32 [32, 3], replicated, may hold values from -2 to 2, as said below
Outputs:
- smeared: bfloat16 [4, 2, 3, 64, 8, 144], P('tm', None, None, None, 'space')
- elementals: bfloat16 [32, 4, 2, 64, 64], P(None, 'tm')
- correlator: float32 [2, 32, 4, 4], P(None, None, 'tm')
Inputs may be any that keep to these rules, and one draw needn't show every extreme that they name: `momenta`: every row is a nonzero vector of integers.
All inputs are finite; a program needn't handle non-finite values.
Results may differ from a plain program's by a relative error of at most 0.0053.
Values may be sent and summed in bfloat16 or wider, within the bound.
A program may use at most 128 MiB of HBM per device.

v0:
```python
import math

import jax
import jax.numpy as jnp
from jax import lax
from jax.sharding import PartitionSpec as P

NEV = 64
LX = 24
YB = 4


KAPPA = 0.25
op_block = 4


def shifted(value, axis, steps):
    count = lax.axis_size(axis)
    pairs = [(source, (source + steps) % count) for source in range(count)]
    return lax.ppermute(value, axis, pairs)


def padded(cells, sides, width):
    for axis, dim in sides:
        count = lax.axis_size(axis)
        head = lax.slice_in_dim(cells, 0, width, axis=dim)
        tail = lax.slice_in_dim(cells, cells.shape[dim] - width, cells.shape[dim], axis=dim)
        cells = jnp.concatenate(
            [
                lax.ppermute(tail, axis, [(i, (i + 1) % count) for i in range(count)]),
                cells,
                lax.ppermute(head, axis, [((i + 1) % count, i) for i in range(count)]),
            ],
            axis=dim,
        )
    return cells


def shift_row(lattice, stride):
    layout = lattice.shape
    planes = lattice.reshape(layout[:-1] + (layout[-1] // LX, LX))
    planes = jnp.roll(planes, -stride, axis=-1)
    return planes.reshape(layout)


def transport(one_link, vector, adjoint):
    link_re = one_link[..., 0, :, :, :, :]
    link_im = one_link[..., 1, :, :, :, :]
    vec_re = vector[..., 0, :, :, :, :]
    vec_im = vector[..., 1, :, :, :, :]
    out_re = 0.0
    out_im = 0.0
    for colour in range(3):
        if adjoint:
            factor_re = link_re[..., colour, :, None, :, :]
            factor_im = -link_im[..., colour, :, None, :, :]
        else:
            factor_re = link_re[..., :, colour, None, :, :]
            factor_im = link_im[..., :, colour, None, :, :]
        source_re = vec_re[..., colour : colour + 1, :, :, :]
        source_im = vec_im[..., colour : colour + 1, :, :, :]
        out_re = out_re + factor_re * source_re - factor_im * source_im
        out_im = out_im + factor_re * source_im + factor_im * source_re
    return jnp.stack([out_re, out_im], axis=-5)


def phases(momenta, z_index, y_start, site_count, z_total):
    site_index = jnp.arange(site_count, dtype=jnp.int32)
    x_coord = site_index % LX
    y_coord = y_start + site_index // LX
    z_coord = z_index + jnp.arange(1, dtype=jnp.int32)
    turn_x = momenta[:, 0, None] * x_coord[None] % LX
    turn_y = momenta[:, 1, None] * y_coord[None] % LX
    turn_z = momenta[:, 2, None] * z_coord[None] % z_total
    angles = (
        2.0
        * math.pi
        * (
            turn_x.astype(jnp.float32)[:, None, :] / LX
            + turn_y.astype(jnp.float32)[:, None, :] / LX
            + turn_z.astype(jnp.float32)[:, :, None] / z_total
        )
    )
    return (jnp.cos(angles), -jnp.sin(angles))


def pair_product(left, right):
    return jnp.einsum("tcazs,ptcbzs->ptab", left, right, preferred_element_type=jnp.float32)


def contract(smeared, cos_part, sin_part, norm_scale):
    smear_re = smeared[:, 0]
    smear_im = smeared[:, 1]
    wide_re = smear_re.astype(jnp.float32)
    wide_im = smear_im.astype(jnp.float32)
    cos_wide = cos_part[:, None, None, None]
    sin_wide = sin_part[:, None, None, None]
    phased_re = (wide_re[None] * cos_wide - wide_im[None] * sin_wide).astype(jnp.bfloat16)
    phased_im = (wide_re[None] * sin_wide + wide_im[None] * cos_wide).astype(jnp.bfloat16)
    elem_re = pair_product(smear_re, phased_re) + pair_product(smear_im, phased_im)
    elem_im = pair_product(smear_re, phased_im) - pair_product(smear_im, phased_re)
    return norm_scale * jnp.stack([elem_re, elem_im], axis=2)


def local(eigvecs, gauge_links, perambulators, momenta):
    spaces = lax.axis_size("space")
    z_total = spaces // YB
    site_count = eigvecs.shape[5]
    row_count = site_count // LX
    block_index = lax.axis_index("space")
    y_block = block_index % YB
    z_index = block_index // YB
    summed = (1.0 - 6.0 * KAPPA) * eigvecs
    link_x = gauge_links[0]
    forward = transport(link_x, shift_row(eigvecs, 1), False)
    behind = shift_row(transport(link_x, eigvecs, True), -1)
    summed = summed + KAPPA * (forward + behind)
    link_y = gauge_links[1]
    link_z = gauge_links[2]
    v_above, ylink_above = shifted((eigvecs, link_y[..., site_count - LX :]), "space", -YB)
    v_below, zlink_below = shifted((eigvecs, link_z), "space", YB)
    back_y = transport(link_y, eigvecs, True)
    back_above = transport(ylink_above, v_above[..., site_count - LX :], True)
    to_lower = jnp.where(y_block == 0, v_below[..., :LX], eigvecs[..., :LX])
    to_upper = jnp.where(y_block == YB - 1, back_above, back_y[..., site_count - LX :])
    payload = jnp.concatenate([to_lower, to_upper], axis=4)
    rim_rows = padded(payload, (("space", 4),), 1)
    row_below = rim_rows[:, :, :, :, 0:1]
    row_above = rim_rows[:, :, :, :, 3:4]
    forward = transport(link_y, jnp.concatenate([eigvecs[..., LX:], row_above], axis=5), False)
    behind = jnp.concatenate([row_below, back_y[..., : site_count - LX]], axis=5)
    summed = summed + KAPPA * (forward + behind)
    forward = transport(link_z, v_above, False)
    behind = transport(zlink_below, v_below, True)
    summed = summed + KAPPA * (forward + behind)
    smeared = summed.astype(jnp.bfloat16)
    op_count = momenta.shape[0]
    cos_all, sin_all = phases(momenta, z_index, y_block * row_count, site_count, z_total)
    norm_scale = 1.0 / math.sqrt(3.0 * z_total * LX * LX)
    group_count = op_count // op_block
    cos_group = cos_all.reshape((group_count, op_block) + cos_all.shape[1:])
    sin_group = sin_all.reshape((group_count, op_block) + sin_all.shape[1:])

    def per_group(phase_pair):
        return contract(smeared, phase_pair[0], phase_pair[1], norm_scale)

    partial_sums = lax.map(per_group, (cos_group, sin_group))
    partial_sums = partial_sums.reshape((op_count,) + partial_sums.shape[2:])
    raw_sums = lax.psum(partial_sums, "space")
    elementals = raw_sums.astype(jnp.bfloat16)
    pair_count = perambulators.shape[3] * perambulators.shape[4]
    item_count = op_count * pair_count
    slot_count = (item_count + spaces - 1) // spaces
    item_ids = block_index * slot_count + jnp.arange(slot_count, dtype=jnp.int32)
    is_valid = (item_ids < item_count).astype(jnp.float32)
    clipped = jnp.minimum(item_ids, item_count - 1)
    op_slots = clipped // pair_count
    pair_slots = clipped % pair_count
    owners = (op_slots[:, None] == jnp.arange(op_count, dtype=jnp.int32)[None]).astype(
        jnp.float32
    ) * is_valid[:, None]
    nearby = jnp.take(elementals, op_slots, axis=0)
    near_wide = nearby.astype(jnp.float32)
    near_re = near_wide[:, :, 0]
    near_im = near_wide[:, :, 1]
    blocks = perambulators.reshape(
        perambulators.shape[:3] + (pair_count,) + perambulators.shape[5:]
    )
    chosen = jnp.take(blocks, pair_slots, axis=3)
    high = lax.Precision.HIGHEST
    remote = jnp.take(lax.all_gather(elementals, "tm", axis=1, tiled=True), op_slots, axis=0)
    tau_re = chosen[:, :, 0]
    tau_im = chosen[:, :, 1]
    far_re = remote[:, :, 0]
    far_im = remote[:, :, 1]
    left_re = (
        jnp.einsum("tnjia,jnba->tnjib", tau_re, far_re, preferred_element_type=jnp.float32)
        + jnp.einsum("tnjia,jnba->tnjib", tau_im, far_im, preferred_element_type=jnp.float32)
    ).astype(jnp.bfloat16)
    left_im = (
        jnp.einsum("tnjia,jnba->tnjib", tau_im, far_re, preferred_element_type=jnp.float32)
        - jnp.einsum("tnjia,jnba->tnjib", tau_re, far_im, preferred_element_type=jnp.float32)
    ).astype(jnp.bfloat16)
    right_re = jnp.einsum(
        "tnjib,tnjkb->tnjik", left_re, tau_re, preferred_element_type=jnp.float32
    ) + jnp.einsum("tnjib,tnjkb->tnjik", left_im, tau_im, preferred_element_type=jnp.float32)
    right_im = jnp.einsum(
        "tnjib,tnjkb->tnjik", left_im, tau_re, preferred_element_type=jnp.float32
    ) - jnp.einsum("tnjib,tnjkb->tnjik", left_re, tau_im, preferred_element_type=jnp.float32)
    corr_re = jnp.einsum("jtab,tnjba->tnj", near_re, right_re, precision=high) - jnp.einsum(
        "jtab,tnjba->tnj", near_im, right_im, precision=high
    )
    corr_im = jnp.einsum("jtab,tnjba->tnj", near_re, right_im, precision=high) + jnp.einsum(
        "jtab,tnjba->tnj", near_im, right_re, precision=high
    )
    traces = jnp.stack([corr_re, corr_im]) / NEV
    contrib = jnp.einsum("rtnj,jp->rptn", traces, owners, precision=high)
    correlator = lax.psum(contrib, "space")
    return (smeared, elementals, correlator)


def solution(mesh):
    return jax.shard_map(
        local,
        mesh=mesh,
        in_specs=(
            P("tm", None, None, None, "space", None),
            P(None, "tm", None, None, None, "space", None),
            P("tm", None, None, None, None, None, None),
            P(),
        ),
        out_specs=(
            P("tm", None, None, None, "space", None),
            P(None, "tm", None, None, None),
            P(None, None, "tm", None),
        ),
        check_vma=False,
    )
```

profile of v0, /device:TPU:0, one launch (start us, length us, event | category | flops | bytes accessed | tf_op | source)
XLA Modules:
  0.0 363.6 jit_solution(16562907411794065391)
XLA Ops:
  8.9 4.0 %collective-permute-start.2 = (f32[1,2,3,3,1,24]{5,4,3,2,1,0:T(1,128)}, f32[1,2,3,3,1,24]{5,4,3,2,1,0:T(1,128)}, u32[]{:S(2)}, u32[]{:S(2)}) collective-permute-start(f32[1,2,3,3,1,24]{5,4,3,2,1,0:T(1,128)} %slice.542), channel_id=1, source_target_pairs={{0,16},{4,20},{8,24},{12,28},{16,0},{20,4},{24,8},{28,12},{1,17},{... | collective-permute-start | bytes 5192 | tf_op jit(solution)/shard_map/ppermute | solution.py:20
  12.9 2.9 collective-permute-start.4
  15.8 2.0 fusion.91
  22.3 1.8 copy.137
  24.0 1.8 copy.138
  74.3 1.8 broadcast_select_fusion
  76.1 3.2 collective-permute-start.1
  85.5 2.5 subtract_bitcast_fusion
  88.0 1.9 fusion.53
  97.4 2.5 fusion.45
  101.0 21.7 %while.10 = (s32[]{:T(128)}, f32[8,4,1,2,64,64]{5,4,3,1,0,2:T(8,128)}, bf16[1,2,3,64,1,144]{5,3,2,4,1,0:T(8,128)(2,1)S(1)}, f32[8,4,1,144]{3,1,2,0:T(4,128)}, f32[8,4,1,144]{3,1,2,0:T(4,128)}, /*index=5*/s32[]{:T(128)}) while((s32[]{:T(128)}, f32[8,4,1,2,64,64]{5,4,3,1,0,2:T(8,128)}, bf16[1,2,3,64,1,144]{5,3,2,4,1,0:T(8,128)(2,1)S(1)}, ...), condition=%wide.region_1.2_spmd, body=%wide.region_0.1_spmd.sunk | while | flops 58546176 | bytes 3782217 | solution.py:147
  122.8 88.5 %all-reduce.1 = bf16[32,1,2,64,64]{4,3,2,1,0:T(8,128)(2,1)} all-reduce(f32[32,1,2,64,64]{4,3,2,1,0:T(8,128)} %bitcast.409), channel_id=1, replica_groups=mesh['space'=8,'tm'=4] {'space'}, use_global_device_ids=true, to_apply=%region_2.3 | all-reduce | flops 262144 | bytes 1572864 | tf_op jit(solution)/shard_map/psum | solution.py:149
  211.3 5.3 %gather_fusion.1 = bf16[64,4,2,64,64]{4,3,2,1,0:T(8,128)(2,1)} fusion(bf16[4,2,16,64,64]{4,3,2,1,0:T(8,128)(2,1)S(1)} %bitcast.405, s32[1024]{0:T(1024)S(1)} %pad_clamp_fusion), kind=kCustom, calls=%fused_computation.1 | custom fusion | bytes 8388864 | tf_op jit(solution)/shard_map/jit(_take)/gather | solution.py:169
  216.7 8.8 %bitcast_select_fusion = bf16[1,4,2,64,64,64]{5,4,3,1,2,0:T(8,128)(2,1)} fusion(bf16[64,4,2,64,64]{4,3,2,1,0:T(8,128)(2,1)} %gather_fusion.1, pred[64]{0:T(512)(128)(4,1)S(1)} %get-tuple-element.219), kind=kLoop, calls=%fused_computation.43 | loop fusion | flops 2097152 | bytes 8388672 | tf_op jit(solution)/shard_map/jit(_take)/select_n | solution.py:169
  226.4 2.2 gather_fusion.2
  228.6 1.8 bitcast_select_fusion.1
  230.4 1.8 fusion.38
  232.3 3.0 copy.139
  235.2 1.8 copy.140
  237.0 8.1 %all-gather.2.cloned.1.call-done = bf16[32,4,2,64,64]{4,3,2,1,0:T(8,128)(2,1)} async-done(((bf16[32,1,2,64,64]{4,3,2,1,0:T(8,128)(2,1)}), bf16[32,4,2,64,64]{4,3,2,1,0:T(8,128)(2,1)}) %all-gather.2.cloned.1.call-update) | async-done | bytes 2097168 | tf_op jit(solution)/shard_map/all_gather | solution.py:171
  245.2 7.7 %gather_fusion = bf16[64,4,2,64,64]{4,3,2,1,0:T(8,128)(2,1)} fusion(bf16[32,4,2,64,64]{4,3,2,1,0:T(8,128)(2,1)} %all-gather.2.cloned.1.call-done, s32[1024]{0:T(1024)S(1)} %pad_clamp_fusion.1), kind=kCustom, calls=%fused_computation | custom fusion | bytes 8388864 | tf_op jit(solution)/shard_map/jit(_take)/gather | solution.py:171
  252.9 7.6 %copy_select_fusion = bf16[64,4,2,64,64]{4,3,0,1,2:T(8,128)(2,1)} fusion(bf16[64,4,2,64,64]{4,3,2,1,0:T(8,128)(2,1)} %gather_fusion, pred[64]{0:T(512)(128)(4,1)S(1)} %get-tuple-element.220), kind=kLoop, calls=%fused_computation.48 | loop fusion | flops 2097152 | bytes 8388672 | tf_op jit(solution)/shard_map/jit(_take)/select_n | solution.py:171
  260.6 9.1 %fusion.31 = f32[4,64,64,64]{3,2,1,0:T(8,128)} fusion(bf16[64,4,2,64,64]{4,3,0,1,2:T(8,128)(2,1)} %copy_select_fusion, bf16[1,4,2,64,64,64]{5,4,3,1,2,0:T(8,128)(2,1)} %bitcast_select_fusion), kind=kOutput, calls=%fused_computation.58 | convolution fusion | flops 134217728 | bytes 12582912 | tf_op jit(solution)/shard_map/tnjia,jnba->tnjib/dot_general | solution.py:177
  269.7 7.7 %fusion.30 = f32[4,64,64,64]{3,2,1,0:T(8,128)} fusion(bf16[64,4,2,64,64]{4,3,0,1,2:T(8,128)(2,1)S(1)} %copy-done.2, bf16[1,4,2,64,64,64]{5,4,3,1,2,0:T(8,128)(2,1)} %bitcast_select_fusion), kind=kOutput, calls=%fused_computation.57 | convolution fusion | flops 134217728 | bytes 12582912 | tf_op jit(solution)/shard_map/tnjia,jnba->tnjib/dot_general | solution.py:181
  277.4 8.1 %fusion.29 = bf16[4,64,64,64]{2,3,1,0:T(8,128)(2,1)S(1)} fusion(f32[4,64,64,64]{3,2,1,0:T(8,128)} %fusion.30, bf16[1,4,2,64,64,64]{5,4,3,1,2,0:T(8,128)(2,1)} %bitcast_select_fusion, bf16[64,4,2,64,64]{4,3,0,1,2:T(8,128)(2,1)} %copy_select_fusion), kind=kOutput, calls=%fused_computation.52 | convolution fusion | flops 136314880 | bytes 18874368 | tf_op jit(solution)/shard_map/tnjia,jnba->tnjib/dot_general | solution.py:182
  285.5 7.8 %fusion.34 = f32[4,64,64,64]{3,2,1,0:T(8,128)} fusion(bf16[4,64,64,64]{2,3,1,0:T(8,128)(2,1)S(1)} %fusion.29, bf16[1,4,2,64,64,64]{5,4,3,1,2,0:T(8,128)(2,1)} %bitcast_select_fusion), kind=kOutput, calls=%fused_computation.61 | convolution fusion | flops 134217728 | bytes 10485760 | tf_op jit(solution)/shard_map/tnjib,tnjkb->tnjik/dot_general | solution.py:187
  293.3 7.8 %fusion.37 = f32[4,64,64,64]{3,2,1,0:T(8,128)} fusion(bf16[4,64,64,64]{2,3,1,0:T(8,128)(2,1)S(1)} %fusion.29, bf16[1,4,2,64,64,64]{5,4,3,1,2,0:T(8,128)(2,1)} %bitcast_select_fusion), kind=kOutput, calls=%fused_computation.64 | convolution fusion | flops 134217728 | bytes 10485760 | tf_op jit(solution)/shard_map/tnjib,tnjkb->tnjik/dot_general | solution.py:186
  301.1 8.4 %fusion.28 = bf16[4,64,64,64]{2,3,1,0:T(8,128)(2,1)S(1)} fusion(f32[4,64,64,64]{3,2,1,0:T(8,128)} %fusion.31, bf16[1,4,2,64,64,64]{5,4,3,1,2,0:T(8,128)(2,1)} %bitcast_select_fusion, bf16[64,4,2,64,64]{4,3,0,1,2:T(8,128)(2,1)} %copy_select_fusion), kind=kOutput, calls=%fused_computation.51 | convolution fusion | flops 136314880 | bytes 18874368 | tf_op jit(solution)/shard_map/tnjia,jnba->tnjib/dot_general | solution.py:178
  309.5 2.1 copy-done.3
  311.5 7.8 %fusion.36 = f32[4,64,64,64]{3,2,1,0:T(8,128)} fusion(bf16[4,64,64,64]{2,3,1,0:T(8,128)(2,1)S(1)} %fusion.28, bf16[1,4,2,64,64,64]{5,4,3,1,2,0:T(8,128)(2,1)} %bitcast_select_fusion), kind=kOutput, calls=%fused_computation.63 | convolution fusion | flops 134217728 | bytes 10485760 | tf_op jit(solution)/shard_map/tnjib,tnjkb->tnjik/dot_general | solution.py:189
  319.3 15.4 %multiply_reduce_fusion.3 = (f32[64,4]{0,1:T(4,128)S(1)}, f32[64,4]{0,1:T(4,128)S(1)}, f32[64,4]{0,1:T(4,128)S(1)}, f32[64,4]{0,1:T(4,128)S(1)}) fusion(f32[64,64,64]{1,2,0:T(8,128)} %copy.139, f32[4,64,64,64]{3,2,1,0:T(8,128)} %fusion.37, f32[64,64,64]{1,2,0:T(8,128)} %copy.140, f32[4,64,64,64]{3,2,1,0:T(8,128)} %fusion.34, f32[4,64,64,64]{3,2,1,0:T(8,128)} %fusion.36, ...), kind=kOutput, calls=%fused_computation.47 | convolution fusion | flops 144702464 | bytes 37752832 | tf_op jit(solution)/shard_map/tnjib,tnjkb->tnjik/dot_general | solution.py:184
  334.8 21.9 %psum.15 = f32[2,32,1,4]{1,3,0,2:T(4,128)} all-reduce(f32[2,32,1,4]{1,3,0,2:T(4,128)S(1)} %convolution_bitcast_fusion.4), channel_id=1, replica_groups=mesh['space'=8,'tm'=4] {'space'}, use_global_device_ids=true, to_apply=%region_3.4 | all-reduce | flops 256 | bytes 2048 | tf_op jit(solution)/shard_map/psum | solution.py:198
  (216 shorter events, 91.6 us)
Async XLA Ops:
  7.2 204.1 %copy-start = (bf16[1,4,2,4,4,64,64]{6,5,4,3,2,1,0:T(8,128)(2,1)S(1)}, bf16[1,4,2,4,4,64,64]{6,5,4,3,2,1,0:T(8,128)(2,1)}, u32[]{:S(2)}) copy-start(bf16[1,4,2,4,4,64,64]{6,5,4,3,2,1,0:T(8,128)(2,1)} %param.8) | copy-start | bytes 3145732
  7.2 35.7 %copy-start.5 = (f32[1,2,3,64,1,144]{5,4,3,2,1,0:T(1,128)S(1)}, f32[1,2,3,64,1,144]{5,4,3,2,1,0:T(1,128)}, u32[]{:S(2)}) copy-start(f32[1,2,3,64,1,144]{5,4,3,2,1,0:T(1,128)} %param.6) | copy-start | bytes 663556
  7.2 238.0 %all-gather.2.cloned.1.call-start = ((), (), s32[]{:S(2)}) async-start(), calls=%async_computation | async-start | bytes 5242880 | tf_op jit(solution)/shard_map/all_gather | solution.py:171
  8.9 48.4 %collective-permute-start.2 = (f32[1,2,3,3,1,24]{5,4,3,2,1,0:T(1,128)}, f32[1,2,3,3,1,24]{5,4,3,2,1,0:T(1,128)}, u32[]{:S(2)}, u32[]{:S(2)}) collective-permute-start(f32[1,2,3,3,1,24]{5,4,3,2,1,0:T(1,128)} %slice.542), channel_id=1, source_target_pairs={{0,16},{4,20},{8,24},{12,28},{16,0},{20,4},{24,8},{28,12},{1,17},{... | collective-permute-start | bytes 5192 | tf_op jit(solution)/shard_map/ppermute | solution.py:20
  12.9 52.2 %collective-permute-start = (f32[1,2,3,64,1,144]{5,4,3,2,1,0:T(1,128)}, f32[1,2,3,64,1,144]{5,4,3,2,1,0:T(1,128)}, u32[]{:S(2)}, u32[]{:S(2)}) collective-permute-start(f32[1,2,3,64,1,144]{5,4,3,2,1,0:T(1,128)} %param.6), channel_id=1, source_target_pairs={{0,16},{4,20},{8,24},{12,28},{16,0},{20,4},{24,8},{28,12},{1,17},{... | collective-permute-start | bytes 663560 | tf_op jit(solution)/shard_map/ppermute | solution.py:20
  12.9 48.6 %collective-permute-start.4 = (f32[1,2,3,3,1,144]{5,4,3,2,1,0:T(1,128)S(1)}, f32[1,2,3,3,1,144]{5,4,3,2,1,0:T(1,128)S(1)}, u32[]{:S(2)}, u32[]{:S(2)}) collective-permute-start(f32[1,2,3,3,1,144]{5,4,3,2,1,0:T(1,128)S(1)} %get-tuple-element.139), channel_id=1, source_target_pairs={{0,16},{4,20},{8,24},{12,28},{16,0},{20,4},{24,8},{28,12},{1,17},{... | collective-permute-start | bytes 31112 | tf_op jit(solution)/shard_map/ppermute | solution.py:20
  28.2 21.6 %copy-start.7 = (f32[1,3,1,1,144]{4,3,2,1,0:T(1,128)S(1)}, f32[1,3,1,1,144]{4,3,2,1,0:T(1,128)}, u32[]{:S(2)}) copy-start(f32[1,3,1,1,144]{4,3,2,1,0:T(1,128)} %get-tuple-element.166) | copy-start | bytes 5188
  28.2 27.3 %copy-start.8 = (f32[1,3,1,1,144]{4,3,2,1,0:T(1,128)S(1)}, f32[1,3,1,1,144]{4,3,2,1,0:T(1,128)}, u32[]{:S(2)}) copy-start(f32[1,3,1,1,144]{4,3,2,1,0:T(1,128)} %get-tuple-element.161) | copy-start | bytes 5188
  72.8 24.6 %collective-permute-start.3 = (f32[1,2,3,64,1,24]{3,5,2,1,4,0:T(8,128)}, f32[1,2,3,64,1,24]{3,5,2,1,4,0:T(8,128)}, u32[]{:S(2)}, u32[]{:S(2)}) collective-permute-start(f32[1,2,3,64,1,24]{3,5,2,1,4,0:T(8,128)} %maximum_select_fusion), channel_id=1, source_target_pairs={{0,4},{4,8},{8,12},{12,16},{16,20},{20,24},{24,28},{28,0},{1,5},{5... | collective-permute-start | bytes 110600 | tf_op jit(solution)/shard_map/ppermute | solution.py:30
  76.1 11.9 %collective-permute-start.1 = (f32[1,2,3,64,1,24]{5,4,3,2,1,0:T(1,128)}, f32[1,2,3,64,1,24]{5,4,3,2,1,0:T(1,128)}, u32[]{:S(2)}, u32[]{:S(2)}) collective-permute-start(f32[1,2,3,64,1,24]{5,4,3,2,1,0:T(1,128)} %broadcast_select_fusion), channel_id=1, source_target_pairs={{4,0},{8,4},{12,8},{16,12},{20,16},{24,20},{28,24},{0,28},{5,1},{9... | collective-permute-start | bytes 110600 | tf_op jit(solution)/shard_map/ppermute | solution.py:32
  216.7 8.9 %copy-start.6 = (bf16[1,2,3,64,1,144]{3,5,2,1,4,0:T(8,128)(2,1)S(1)}, bf16[1,2,3,64,1,144]{3,5,2,1,4,0:T(8,128)(2,1)}, u32[]{:S(2)}) copy-start(bf16[1,2,3,64,1,144]{3,5,2,1,4,0:T(8,128)(2,1)} %fusion.45) | copy-start | bytes 331780
  216.7 9.7 %copy-start.4 = (bf16[32,1,2,64,64]{4,3,2,1,0:T(8,128)(2,1)S(1)}, bf16[32,1,2,64,64]{4,3,2,1,0:T(8,128)(2,1)}, u32[]{:S(2)}) copy-start(bf16[32,1,2,64,64]{4,3,2,1,0:T(8,128)(2,1)} %all-reduce.1) | copy-start | bytes 1572868
  260.6 9.1 %copy-start.2 = (bf16[64,4,2,64,64]{4,3,0,1,2:T(8,128)(2,1)S(1)}, bf16[64,4,2,64,64]{4,3,0,1,2:T(8,128)(2,1)}, u32[]{:S(2)}) copy-start(bf16[64,4,2,64,64]{4,3,0,1,2:T(8,128)(2,1)} %copy_select_fusion) | copy-start | bytes 12582916
  309.5 2.1 copy-start.3
  319.3 37.5 %copy-start.1 = (bf16[1,4,2,4,4,64,64]{6,5,4,3,2,1,0:T(8,128)(2,1)S(1)}, bf16[1,4,2,4,4,64,64]{6,5,4,3,2,1,0:T(8,128)(2,1)}, u32[]{:S(2)}) copy-start(bf16[1,4,2,4,4,64,64]{6,5,4,3,2,1,0:T(8,128)(2,1)} %param.8) | copy-start | bytes 3145732
Sparse Core Ops, SparseCore 0:
  211.4 33.7 all-gather.1
where the time goes:
time: 366 us; the launch traced here: 364 us
  blocking collectives  110 us (30%)
  local copies, waits for them, and re-layouts  97.8 us (27%)
  matrix products  80.5 us (22%)
  other arithmetic  40.1 us (11%)
  between operations  14.4 us (4%)
  starting transfers between devices  11.7 us (3%)
  waiting for transfers between devices  8.15 us (2%)
    psum x1, blocking collectives, local(): raw_sums = lax.psum(partial_sums, 'space')  88.5 us
    unnamed x60, local copies, waits for them, and re-layouts  37.4 us
    psum x1, blocking collectives, local(): correlator = lax.psum(contrib, 'space')  21.9 us
    dot_general x1, matrix products, local(): jnp.einsum('tnjib,tnjkb->tnjik', left_re, tau_re, preferred_element_type=...  15.4 us
    mul x24, local copies, waits for them, and re-layouts, transport(): out_re = out_re + factor_re * source_re - factor_im * source_im  14.2 us
    dot_general x1, matrix products, local(): jnp.einsum('tnjia,jnba->tnjib', tau_re, far_re, preferred_element_type=jn...  9.1 us
    select_n x2, other arithmetic, local(): chosen = jnp.take(blocks, pair_slots, axis=3)  8.85 us
    dot_general x32, matrix products, pair_product(): jnp.einsum('tcazs,ptcbzs->ptab', left, right, preferred_element_type=jnp....  8.39 us
  transfers between devices with their start and end apart: 6, of which 1 were waited for; matrix products, arithmetic and copies ran while one was open for 26% of the time, Pallas kernels for 0%

commit v1 on v0

v1 whole, which is shorter than its diff:
```python
import functools
import math

import jax
import jax.numpy as jnp
from jax import lax
from jax.experimental import pallas as pl
from jax.experimental.pallas import tpu as pltpu
from jax.sharding import PartitionSpec as P

LX = 24
YB = 4
KAPPA = 0.25
VMEM_LIMIT = 40 * 1024 * 1024
NT_DIMS = (((1,), (1,)), ((), ()))


def phases(momenta, z_index, y_start, site_count, z_total):
    site_index = jnp.arange(site_count, dtype=jnp.int32)
    x_coord = site_index % LX
    y_coord = y_start + site_index // LX
    turn_x = momenta[:, 0, None] * x_coord[None] % LX
    turn_y = momenta[:, 1, None] * y_coord[None] % LX
    turn_z = momenta[:, 2, None] * z_index % z_total
    angles = (
        2.0
        * math.pi
        * (
            turn_x.astype(jnp.float32) / LX
            + turn_y.astype(jnp.float32) / LX
            + turn_z.astype(jnp.float32) / z_total
        )
    )
    return jnp.cos(angles), -jnp.sin(angles)


def link_times(link, vector, adjoint):
    real, imag = [], []
    for row in range(3):
        out_re = out_im = None
        for colour in range(3):
            k = colour * 3 + row if adjoint else row * 3 + colour
            a, b = link(k), link(9 + k)
            if adjoint:
                b = -b
            x, y = vector(colour), vector(3 + colour)
            term_re = a * x - b * y
            term_im = a * y + b * x
            out_re = term_re if out_re is None else out_re + term_re
            out_im = term_im if out_im is None else out_im + term_im
        real.append(out_re)
        imag.append(out_im)
    return real + imag


def signed_roll(block, sign_low):
    half = block.shape[-1] // 2
    lane = lax.broadcasted_iota(jnp.int32, block.shape, 1)
    turned = pltpu.roll(block, half, 1)
    low = lane < half
    return jnp.where(low, sign_low * turned, -sign_low * turned)


def smear_kernel(
    norm_scale, v, up, down, u, zb, ra, rb, cs, sn, sm, elem, pad, wide, rows, sums
):
    nev, sites = v.shape[1], v.shape[2]
    lanes = pad.shape[2]
    lane = lax.broadcasted_iota(jnp.int32, (nev, lanes), 1)
    x_coord = lane % LX
    for i in range(6):
        pad[i, :, :sites] = v[i]
        sums[i] = (1.0 - 6.0 * KAPPA) * v[i]

    def add(terms):
        for i in range(6):
            sums[i] = sums[i] + KAPPA * terms[i]

    def link(d):
        return lambda k: u[d, k : k + 1, :]

    def forward_x(i):
        full = pad[i]
        return jnp.where(
            x_coord == LX - 1, pltpu.roll(full, LX - 1, 1), pltpu.roll(full, lanes - 1, 1)
        )[:, :sites]

    def forward_y(i):
        full = pad[i]
        return jnp.where(
            lane >= sites - LX,
            pltpu.roll(rows[i], sites - LX, 1),
            pltpu.roll(full, lanes - LX, 1),
        )[:, :sites]

    for i in range(6):
        rows[i, :, :LX] = ra[i].astype(jnp.float32)
    add(link_times(link(0), forward_x, False))
    add(link_times(link(1), forward_y, False))
    add(link_times(link(2), lambda i: up[i].astype(jnp.float32), False))
    add(link_times(lambda k: zb[k : k + 1, :], lambda i: down[i].astype(jnp.float32), True))
    for i, term in enumerate(link_times(link(0), lambda i: v[i], True)):
        pad[i, :, :sites] = term
    add(
        [
            jnp.where(
                x_coord == 0, pltpu.roll(pad[i], lanes - LX + 1, 1), pltpu.roll(pad[i], 1, 1)
            )[:, :sites]
            for i in range(6)
        ]
    )
    for i, term in enumerate(link_times(link(1), lambda i: v[i], True)):
        pad[i, :, :sites] = term
    for i in range(6):
        rows[i, :, :LX] = rb[i].astype(jnp.float32)
    add(
        [
            jnp.where(lane < LX, rows[i], pltpu.roll(pad[i], LX, 1))[:, :sites]
            for i in range(6)
        ]
    )
    for i in range(6):
        rounded = sums[i].astype(jnp.bfloat16)
        sm[i] = rounded
        wide[i] = rounded.astype(jnp.float32)

    per = 2 if elem.shape[0] % 2 == 0 else 1

    def step(g, carry):
        product = None
        for colour in range(3):
            s_re, s_im = wide[colour], wide[3 + colour]
            parts = []
            for j in range(per):
                cos_row = cs[pl.ds(g * per + j, 1), :]
                sin_row = sn[pl.ds(g * per + j, 1), :]
                parts.append((s_re * cos_row - s_im * sin_row).astype(jnp.bfloat16))
                parts.append((s_re * sin_row + s_im * cos_row).astype(jnp.bfloat16))
            left = jnp.concatenate([sm[colour], sm[3 + colour]], axis=0)
            term = lax.dot_general(
                left, jnp.concatenate(parts, axis=0), NT_DIMS, preferred_element_type=jnp.float32
            )
            product = term if product is None else product + term
        for j in range(per):
            block = product[:, j * 2 * nev : (j + 1) * 2 * nev]
            elem[g * per + j] = norm_scale * (block[:nev] + signed_roll(block[nev:], 1.0))
        return carry

    lax.fori_loop(0, elem.shape[0] // per, step, 0)


def trace_kernel(far, bc, g_re, g_im, out, left, b2, weights):
    ops = far.shape[1]
    nev, width = far.shape[2], far.shape[3]
    pairs = bc.shape[1] // nev
    for p in range(ops):
        block = far[0, p].astype(jnp.float32)
        weights[2 * p * nev : (2 * p + 1) * nev, :] = far[0, p]
        weights[(2 * p + 1) * nev : (2 * p + 2) * nev, :] = signed_roll(block, -1.0).astype(
            jnp.bfloat16
        )
    left[...] = lax.dot_general(
        bc[0], weights[...], NT_DIMS, preferred_element_type=jnp.float32
    ).astype(jnp.bfloat16)
    b2[...] = signed_roll(bc[0].astype(jnp.float32), -1.0).astype(jnp.bfloat16)
    right = None
    for q in range(0, pairs, 2):
        spans = [slice(k * nev, (k + 1) * nev) for k in (q, q + 1)]
        stacked = jnp.concatenate(
            [
                jnp.concatenate([left[s, p * width : (p + 1) * width] for s in spans], axis=1)
                for p in range(ops)
            ],
            axis=0,
        )
        facing = jnp.concatenate(
            [
                jnp.concatenate([bc[0, s, :] for s in spans], axis=1),
                jnp.concatenate([b2[s, :] for s in spans], axis=1),
            ],
            axis=0,
        )
        term = lax.dot_general(stacked, facing, NT_DIMS, preferred_element_type=jnp.float32)
        right = term if right is None else right + term
    for part, g in enumerate((g_re, g_im)):
        for p in range(ops):
            total = jnp.sum(g[p] * right[p * nev : (p + 1) * nev], keepdims=True) / nev
            out[0, part * ops + p : part * ops + p + 1, :] = jnp.broadcast_to(total, (1, width))


def local(eigvecs, gauge_links, perambulators, momenta):
    spaces = lax.axis_size("space")
    z_total = spaces // YB
    nev, sites = eigvecs.shape[3], eigvecs.shape[5]
    block_index = lax.axis_index("space")
    y_block = block_index % YB
    z_index = block_index // YB
    op_count = momenta.shape[0]
    v = eigvecs.reshape(6, nev, sites)
    u = gauge_links.reshape(3, 18, sites)

    def along(value, z_steps, y_steps):
        pairs = []
        for s in range(spaces):
            z, y = s // YB, s % YB
            pairs.append((s, (z + z_steps) % z_total * YB + (y + y_steps) % YB))
        return lax.ppermute(value, "space", pairs)

    narrow = v.astype(jnp.bfloat16)
    up = along(narrow, -1, 0)
    down = up if z_total == 2 else along(narrow, 1, 0)
    zlink = along(u[2], 1, 0)
    edge = jnp.stack(
        link_times(
            lambda k: u[1, k : k + 1, sites - LX :], lambda i: v[i, :, sites - LX :], True
        )
    )
    row_above = along(v[:, :, :LX], 0, -1)
    row_below = along(edge, 0, 1)
    cos_all, sin_all = phases(momenta, z_index, y_block * (sites // LX), sites, z_total)
    t_all = perambulators.shape[1]
    pair_count = perambulators.shape[3] * perambulators.shape[4]
    blocks = perambulators.reshape(t_all, 2, pair_count * nev, nev)
    both = jnp.concatenate([blocks[:, 0], blocks[:, 1]], axis=2)

    lanes = -(-sites // 128) * 128
    smeared, partial_sums = pl.pallas_call(
        functools.partial(smear_kernel, 1.0 / math.sqrt(3.0 * z_total * LX * LX)),
        out_shape=(
            jax.ShapeDtypeStruct((6, nev, sites), jnp.bfloat16),
            jax.ShapeDtypeStruct((op_count, nev, 2 * nev), jnp.float32),
        ),
        scratch_shapes=[
            pltpu.VMEM((6, nev, lanes), jnp.float32),
            pltpu.VMEM((6, nev, sites), jnp.float32),
            pltpu.VMEM((6, nev, lanes), jnp.float32),
            pltpu.VMEM((6, nev, sites), jnp.float32),
        ],
        compiler_params=pltpu.CompilerParams(vmem_limit_bytes=VMEM_LIMIT),
        name="smear",
    )(v, up, down, u, zlink, row_above, row_below, cos_all, sin_all)

    if op_count % spaces == 0:
        own = lax.psum_scatter(partial_sums, "space", scatter_dimension=0, tiled=True)
        own = own.astype(jnp.bfloat16)
        every = lax.all_gather(own, "space", axis=0, tiled=True)
    else:
        every = lax.psum(partial_sums, "space").astype(jnp.bfloat16)
        slots = -(-op_count // spaces)
        ids = jnp.minimum(block_index * slots + jnp.arange(slots), op_count - 1)
        own = jnp.take(every, ids, axis=0)
    ops = own.shape[0]
    far = lax.all_gather(own, "tm", axis=0)
    wide = own.astype(jnp.float32)
    near_re = jnp.swapaxes(wide[:, :, :nev], 1, 2)
    near_im = jnp.swapaxes(wide[:, :, nev:], 1, 2)
    g_re = jnp.concatenate([near_re, -near_im], axis=2)
    g_im = jnp.concatenate([near_im, near_re], axis=2)
    width = 2 * nev
    traces = pl.pallas_call(
        trace_kernel,
        grid=(t_all,),
        out_shape=jax.ShapeDtypeStruct((t_all, 2 * ops, width), jnp.float32),
        in_specs=[
            pl.BlockSpec((1, ops, nev, width), lambda t: (t, 0, 0, 0)),
            pl.BlockSpec((1, pair_count * nev, width), lambda t: (t, 0, 0)),
            pl.BlockSpec((ops, nev, width), lambda t: (0, 0, 0)),
            pl.BlockSpec((ops, nev, width), lambda t: (0, 0, 0)),
        ],
        out_specs=pl.BlockSpec((1, 2 * ops, width), lambda t: (t, 0, 0)),
        scratch_shapes=[
            pltpu.VMEM((pair_count * nev, ops * width), jnp.bfloat16),
            pltpu.VMEM((pair_count * nev, width), jnp.bfloat16),
            pltpu.VMEM((ops * width, width), jnp.bfloat16),
        ],
        compiler_params=pltpu.CompilerParams(vmem_limit_bytes=VMEM_LIMIT),
        name="traces",
    )(far, both, g_re, g_im)
    terms = lax.all_gather(traces[:, :, 0].reshape(t_all, 2, ops), "space", axis=0)
    terms = jnp.transpose(terms, (2, 0, 3, 1)).reshape(2, spaces * ops, t_all)
    correlator = terms[:, :op_count, None, :]
    elementals = jnp.swapaxes(every.reshape(op_count, nev, 2, nev), 1, 2)[:, None]
    return (smeared.reshape(eigvecs.shape), elementals, correlator)


def solution(mesh):
    return jax.shard_map(
        local,
        mesh=mesh,
        in_specs=(
            P("tm", None, None, None, "space", None),
            P(None, "tm", None, None, None, "space", None),
            P("tm", None, None, None, None, None, None),
            P(),
        ),
        out_specs=(
            P("tm", None, None, None, "space", None),
            P(None, "tm", None, None, None),
            P(None, None, "tm", None),
        ),
        check_vma=False,
    )
```

time: 366 us -> 189 us (0.52)
  local copies, waits for them, and re-layouts: 97.8 us -> 6.78 us
  matrix products: 80.5 us -> 0 us
  waiting for transfers between devices: 8.15 us -> 75.7 us
  blocking collectives: 110 us -> 67.5 us
  other arithmetic: 40.1 us -> 3.76 us
  Pallas kernels: 0 us -> 13.3 us
  starting transfers between devices: 11.7 us -> 7.25 us
    psum x2 -> x0, blocking collectives: 110 us -> none  [the longest x1 88.5 us: local(): raw_sums = lax.psum(partial_sums, 'space')]
    dot_general x41 -> x0, matrix products: 80.5 us -> none  [the longest x1 15.4 us: local(): jnp.einsum('tnjib,tnjkb->tnjik', left_re, tau_re, preferred_element_type=...]
    reduce_scatter x0 -> x1, waiting for transfers between devices: none -> 71 us  [local(): lax.psum_scatter(partial_sums, 'space', scatter_dimension=0, tiled=True)]
    all_gather x0 -> x3, blocking collectives: none -> 67.5 us  [the longest x1 31.4 us: local(): every = lax.all_gather(own, 'space', axis=0, tiled=True)]
    unnamed x60 -> x6, local copies, waits for them, and re-layouts: 37.4 us -> 1.2 us
    select_n x8 -> x0, other arithmetic: 20.8 us -> none  [the longest x2 8.85 us: local(): chosen = jnp.take(blocks, pair_slots, axis=3)]
    mul x33 -> x0, local copies, waits for them, and re-layouts: 20.4 us -> none  [the longest x24 14.2 us: transport(): out_re = out_re + factor_re * source_re - factor_im * source_im]
    gather x3 -> x0, local copies, waits for them, and re-layouts: 15.2 us -> none  [the longest x1 7.73 us: local(): jnp.take(lax.all_gather(elementals, 'tm', axis=1, tiled=True), op_slots,...]
  transfers between devices with their start and end apart: 6 -> 5, of which waited for: 1 -> 2; matrix products, arithmetic and copies ran while one was open for 26% -> 1% of each run, Pallas kernels for 0% -> 0%
where the time goes in v1:
time: 189 us
  waiting for transfers between devices  75.7 us (40%)
  blocking collectives  67.5 us (36%)
  between operations  14.3 us (8%)
  Pallas kernels  13.3 us (7%)
  starting transfers between devices  7.25 us (4%)
  local copies, waits for them, and re-layouts  6.78 us (4%)
  other arithmetic  3.76 us (2%)
    reduce_scatter x1, waiting for transfers between devices, local(): lax.psum_scatter(partial_sums, 'space', scatter_dimension=0, tiled=True)  71 us
    all_gather x1, blocking collectives, local(): every = lax.all_gather(own, 'space', axis=0, tiled=True)  31.4 us
    all_gather x1, blocking collectives, local(): lax.all_gather(traces[:, :, 0].reshape(t_all, 2, ops), 'space', axis=0)  30.4 us
    pallas_call x1, Pallas kernels, local(): pl.pallas_call(functools.partial(smear_kernel, 1.0 / math.sqrt(3.0 * z_to...  7.89 us
    ppermute x4, starting transfers between devices, along(): return lax.ppermute(value, 'space', pairs)  7.21 us
    all_gather x1, blocking collectives, local(): far = lax.all_gather(own, 'tm', axis=0)  5.79 us
    pallas_call x1, Pallas kernels, local(): pl.pallas_call(trace_kernel, grid=(t_all,), out_shape=jax.ShapeDtypeStruc...  5.44 us
    ppermute x4, waiting for transfers between devices, along(): return lax.ppermute(value, 'space', pairs)  4.73 us
  transfers between devices with their start and end apart: 5, of which 2 were waited for; matrix products, arithmetic and copies ran while one was open for 1% of the time, Pallas kernels for 0%

profile of v1, /device:TPU:0, one launch (start us, length us, event | category | flops | bytes accessed | tf_op | source)
XLA Modules:
  0.0 188.6 jit_solution(17828635157368882265)
XLA Ops:
  7.2 1.0 reduce
  8.2 0.1 fusion.21
  8.3 1.0 copy.59
  9.4 0.1 add_dynamic-update-slice_fusion.5
  9.5 0.1 add_dynamic-update-slice_fusion.4
  9.6 0.1 add_dynamic-update-slice_fusion.3
  9.7 0.1 add_dynamic-update-slice_fusion.2
  9.9 0.1 add_dynamic-update-slice_fusion.1
  10.0 0.1 add_dynamic-update-slice_fusion
  10.1 3.0 %collective-permute-start.3 = (f32[6,64,24]{2,1,0:T(8,128)S(1)}, f32[6,64,24]{2,1,0:T(8,128)S(1)}, u32[]{:S(2)}, u32[]{:S(2)}) collective-permute-start(f32[6,64,24]{2,1,0:T(8,128)S(1)} %add_dynamic-update-slice_fusion), channel_id=1, source_target_pairs={{0,4},{4,8},{8,12},{12,0},{16,20},{20,24},{24,28},{28,16},{1,5},{5... | collective-permute-start | bytes 110600 | tf_op jit(solution)/shard_map/ppermute | solution.py:207
  13.1 1.1 collective-permute-start.2
  14.2 3.1 %collective-permute-start = (bf16[6,64,144]{2,1,0:T(8,128)(2,1)S(1)}, bf16[6,64,144]{2,1,0:T(8,128)(2,1)S(1)}, u32[]{:S(2)}, u32[]{:S(2)}) collective-permute-start(bf16[6,64,144]{2,1,0:T(8,128)(2,1)S(1)} %bitcast_convert_fusion), channel_id=1, source_target_pairs={{0,16},{4,20},{8,24},{12,28},{16,0},{20,4},{24,8},{28,12},{1,17},{... | collective-permute-start | bytes 331784 | tf_op jit(solution)/shard_map/ppermute | solution.py:207
  17.3 0.8 slice_reduce_fusion
  18.3 0.2 sine_negate_fusion
  18.5 4.7 %collective-permute-done.1.zb = f32[18,144]{1,0:T(8,128)S(1)} collective-permute-done((f32[18,144]{1,0:T(8,128)S(1)}, f32[18,144]{1,0:T(8,128)S(1)}, u32[]{:S(2)}, u32[]{:S(2)}) %collective-permute-start.1) | collective-permute-done | bytes 10400 | tf_op jit(solution)/shard_map/ppermute | solution.py:207
  23.2 7.9 %smear.1 = (bf16[6,64,144]{2,1,0:T(8,128)(2,1)}, f32[32,64,128]{2,1,0:T(8,128)S(1)}) custom-call(f32[6,64,144]{2,1,0:T(8,128)S(1)} %bitcast.77, bf16[6,64,144]{2,1,0:T(8,128)(2,1)S(1)} %collective-permute-done.up.down, bf16[6,64,144]{2,1,0:T(8,128)(2,1)S(1)} %collective-permute-done.up.down, f32[3,18,144]{2,1,0:T(8,128)S(1)} %reshape.342.u, ...), custom_call_target="tpu_custom_call" | custom-call | tf_op jit(solution)/shard_map/smear/pallas_call | solution.py:227
  31.1 2.0 %copy.50 = f32[32,64,128]{1,2,0:T(8,128)} copy(f32[32,64,128]{2,1,0:T(8,128)S(1)} %get-tuple-element.6) | data formatting | bytes 2097152 | tf_op jit(solution)/shard_map/smear/pallas_call | solution.py:227
  33.1 0.2 copy.54
  33.3 0.1 slice_bitcast_fusion.1
  33.4 0.6 pad_maximum_fusion.bc
  34.0 71.0 %reduce-scatter.2.cloned.1.call-done = f32[4,64,128]{1,2,0:T(8,128)} async-done(((f32[32,64,128]{1,2,0:T(8,128)}), f32[4,64,128]{1,2,0:T(8,128)}) %reduce-scatter.2.cloned.1.call-update) | async-done | bytes 131088 | tf_op jit(solution)/shard_map/reduce_scatter | solution.py:244
  105.0 1.0 fusion.29
  106.0 0.1 copy.51
  106.1 5.8 %all-gather = bf16[16,64,128]{2,1,0:T(8,128)(2,1)S(1)} all-gather(bf16[4,64,128]{2,1,0:T(8,128)(2,1)S(1)} %copy.51), channel_id=2, replica_groups=mesh['space'=8,'tm'=4] {'tm'}, dimensions={0}, use_global_device_ids=true | all-gather | bytes 327680 | tf_op jit(solution)/shard_map/all_gather | solution.py:253
  111.9 31.4 %all_gather.12 = bf16[32,64,128]{2,1,0:T(8,128)(2,1)S(1)} all-gather(bf16[4,64,128]{2,1,0:T(8,128)(2,1)S(1)} %copy.51), channel_id=1, replica_groups=mesh['space'=8,'tm'=4] {'space'}, dimensions={0}, use_global_device_ids=true | all-gather | bytes 589824 | tf_op jit(solution)/shard_map/all_gather | solution.py:246
  143.3 0.1 pad_maximum_fusion.2
  143.4 5.4 %traces.1 = f32[4,8,128]{2,1,0:T(8,128)S(1)} custom-call(bf16[4,4,64,128]{3,2,1,0:T(8,128)(2,1)S(1)} %bitcast.78, bf16[4,1024,128]{2,1,0:T(8,128)(2,1)S(1)} %pad_maximum_fusion.bc, f32[4,64,128]{2,1,0:T(8,128)S(1)} %get-tuple-element.29.g_re, f32[4,64,128]{2,1,0:T(8,128)S(1)} %get-tuple-element.28.g_im), custom_call_target="tpu_custom_call" | custom-call | tf_op jit(solution)/shard_map/traces/pallas_call | solution.py:260
  148.9 0.1 slice_reduce_fusion.1
  149.1 30.4 %all_gather.15 = f32[8,4,2,4]{3,1,2,0:T(4,128)S(1)} all-gather(f32[1,4,2,4]{3,1,2,0:T(4,128)S(1)} %copy.55), channel_id=1, replica_groups=mesh['space'=8,'tm'=4] {'space'}, dimensions={0}, use_global_device_ids=true | all-gather | bytes 1152 | tf_op jit(solution)/shard_map/all_gather | solution.py:279
  179.5 0.7 broadcast_in_dim_reshape.3
  180.1 0.4 reshape.344
  180.6 1.2 copy.63
  (22 shorter events, 0.4 us)
Async XLA Ops:
  7.2 11.0 %copy-start.1 = (s32[32,3]{0,1:T(4,128)S(1)}, s32[32,3]{0,1:T(4,128)}, u32[]{:S(2)}) copy-start(s32[32,3]{0,1:T(4,128)} %param.7) | copy-start | bytes 1156
  7.2 97.8 %reduce-scatter.2.cloned.1.call-start = ((), (), s32[]{:S(2)}) async-start(), calls=%async_computation.1 | async-start | bytes 2359296 | tf_op jit(solution)/shard_map/reduce_scatter | solution.py:244
  10.1 13.1 %collective-permute-start.3 = (f32[6,64,24]{2,1,0:T(8,128)S(1)}, f32[6,64,24]{2,1,0:T(8,128)S(1)}, u32[]{:S(2)}, u32[]{:S(2)}) collective-permute-start(f32[6,64,24]{2,1,0:T(8,128)S(1)} %add_dynamic-update-slice_fusion), channel_id=1, source_target_pairs={{0,4},{4,8},{8,12},{12,0},{16,20},{20,24},{24,28},{28,16},{1,5},{5... | collective-permute-start | bytes 110600 | tf_op jit(solution)/shard_map/ppermute | solution.py:207
  13.1 10.1 %collective-permute-start.2 = (f32[6,64,24]{2,1,0:T(8,128)S(1)}, f32[6,64,24]{2,1,0:T(8,128)S(1)}, u32[]{:S(2)}, u32[]{:S(2)}) collective-permute-start(f32[6,64,24]{2,1,0:T(8,128)S(1)} %slice.149), channel_id=1, source_target_pairs={{0,12},{4,0},{8,4},{12,8},{16,28},{20,16},{24,20},{28,24},{1,13},{... | collective-permute-start | bytes 110600 | tf_op jit(solution)/shard_map/ppermute | solution.py:207
  14.2 9.0 %collective-permute-start = (bf16[6,64,144]{2,1,0:T(8,128)(2,1)S(1)}, bf16[6,64,144]{2,1,0:T(8,128)(2,1)S(1)}, u32[]{:S(2)}, u32[]{:S(2)}) collective-permute-start(bf16[6,64,144]{2,1,0:T(8,128)(2,1)S(1)} %bitcast_convert_fusion), channel_id=1, source_target_pairs={{0,16},{4,20},{8,24},{12,28},{16,0},{20,4},{24,8},{28,12},{1,17},{... | collective-permute-start | bytes 331784 | tf_op jit(solution)/shard_map/ppermute | solution.py:207
  18.1 5.1 %collective-permute-start.1 = (f32[18,144]{1,0:T(8,128)S(1)}, f32[18,144]{1,0:T(8,128)S(1)}, u32[]{:S(2)}, u32[]{:S(2)}) collective-permute-start(f32[18,144]{1,0:T(8,128)S(1)} %squeeze.6), channel_id=1, source_target_pairs={{0,16},{4,20},{8,24},{12,28},{16,0},{20,4},{24,8},{28,12},{1,17},{... | collective-permute-start | bytes 31112 | tf_op jit(solution)/shard_map/ppermute | solution.py:207
  31.1 2.0 %copy-start = (bf16[1,4,2,4,4,64,64]{6,5,4,3,2,1,0:T(8,128)(2,1)S(1)}, bf16[1,4,2,4,4,64,64]{6,5,4,3,2,1,0:T(8,128)(2,1)}, u32[]{:S(2)}) copy-start(bf16[1,4,2,4,4,64,64]{6,5,4,3,2,1,0:T(8,128)(2,1)} %param.6) | copy-start | bytes 3145732
Sparse Core Ops, SparseCore 0:
  33.2 71.7 reduce-scatter.1

commit v2 on v1

--- a/solution.py
+++ b/solution.py
@@ -188,6 +188,157 @@
             out[0, part * ops + p : part * ops + p + 1, :] = jnp.broadcast_to(total, (1, width))
 
 
+def exchange_kernel(
+    spaces, slices, partial, bc, every, gathered, inbox, far, left, b2, weights, tile, send, recv
+):
+    me, mine = lax.axis_index("space"), lax.axis_index("tm")
+    ops, nev, width = inbox.shape[1:]
+    pairs = bc.shape[1] // nev
+
+    barrier = pltpu.get_barrier_semaphore()
+    for d in range(1, spaces):
+        pl.semaphore_signal(
+            barrier, inc=1, device_id=((me + d) % spaces, mine), device_id_type=pl.DeviceIdType.MESH
+        )
+    for d in range(1, slices):
+        pl.semaphore_signal(
+            barrier, inc=1, device_id=(me, (mine + d) % slices), device_id_type=pl.DeviceIdType.MESH
+        )
+    pl.semaphore_wait(barrier, spaces + slices - 2)
+
+    def to_space(kind, d, source, target):
+        return pltpu.make_async_remote_copy(
+            src_ref=source,
+            dst_ref=target,
+            send_sem=send.at[kind, d],
+            recv_sem=recv.at[kind, d],
+            device_id=((me + d) % spaces, mine),
+            device_id_type=pl.DeviceIdType.MESH,
+        )
+
+    def to_slice(d, source, target):
+        return pltpu.make_async_remote_copy(
+            src_ref=source,
+            dst_ref=target,
+            send_sem=send.at[3, d],
+            recv_sem=recv.at[3, d],
+            device_id=(me, (mine + d) % slices),
+            device_id_type=pl.DeviceIdType.MESH,
+        )
+
+    sums = [
+        to_space(0, d, partial.at[pl.ds((me + d) % spaces * ops, ops)], inbox.at[d])
+        for d in range(1, spaces)
+    ]
+    for copy in sums:
+        copy.start()
+    b2[...] = signed_roll_3d(bc)
+    total = partial[pl.ds(me * ops, ops)]
+    for d, copy in enumerate(sums, 1):
+        copy.wait_recv()
+        total = total + inbox[d]
+    rounded = total.astype(jnp.bfloat16)
+    far[mine] = rounded
+    every[pl.ds(me * ops, ops)] = rounded
+    fars = [to_slice(d, far.at[mine], far.at[mine]) for d in range(1, slices)]
+    for copy in fars:
+        copy.start()
+    shares = [
+        to_space(1, d, far.at[mine], every.at[pl.ds(me * ops, ops)]) for d in range(1, spaces)
+    ]
+    for copy in shares:
+        copy.start()
+
+    near = rounded.astype(jnp.float32)
+    low = lax.broadcasted_iota(jnp.int32, (nev, width), 1) < nev
+    near_re, near_im = [], []
+    for p in range(0, ops, 2):
+        one, two = near[p], near[p + 1]
+        near_re.append(jnp.where(low, one, pltpu.roll(two, nev, 1)))
+        near_im.append(jnp.where(low, pltpu.roll(one, nev, 1), two))
+    near_re = jnp.concatenate(near_re, axis=1)
+    near_im = jnp.concatenate(near_im, axis=1)
+    row_id = lax.broadcasted_iota(jnp.int32, (2 * ops, width), 0)
+    lane_id = lax.broadcasted_iota(jnp.int32, (2 * ops, width), 1)
+    low_row = lax.broadcasted_iota(jnp.int32, (1, width), 1) < nev
+    tile[...] = jnp.zeros_like(tile)
+
+    def step(d, carry):
+        @pl.when(d > 0)
+        def _():
+            pltpu.make_async_remote_copy(
+                src_ref=far.at[mine],
+                dst_ref=far.at[mine],
+                send_sem=send.at[3, d],
+                recv_sem=recv.at[3, d],
+                device_id=(me, (mine + d) % slices),
+                device_id_type=pl.DeviceIdType.MESH,
+            ).wait_recv()
+
+        t0 = (mine + slices - d) % slices
+        for p in range(ops):
+            block = far[t0, p]
+            weights[2 * p * nev : (2 * p + 1) * nev, :] = block
+            weights[(2 * p + 1) * nev : (2 * p + 2) * nev, :] = signed_roll(
+                block.astype(jnp.float32), -1.0
+            ).astype(jnp.bfloat16)
+        left[...] = lax.dot_general(
+            bc[t0], weights[...], NT_DIMS, preferred_element_type=jnp.float32
+        ).astype(jnp.bfloat16)
+        right = None
+        for q in range(0, pairs, 2):
+            spans = [slice(k * nev, (k + 1) * nev) for k in (q, q + 1)]
+            stacked = jnp.concatenate(
+                [
+                    jnp.concatenate([left[s, p * width : (p + 1) * width] for s in spans], axis=1)
+                    for p in range(ops)
+                ],
+                axis=0,
+            )
+            facing = jnp.concatenate(
+                [
+                    jnp.concatenate([bc[t0, s, :] for s in spans], axis=1),
+                    jnp.concatenate([b2[t0, s, :] for s in spans], axis=1),
+                ],
+                axis=0,
+            )
+            term = lax.dot_general(facing, stacked, NT_DIMS, preferred_element_type=jnp.float32)
+            right = term if right is None else right + term
+        r_re, r_im = right[:nev], right[nev:]
+        rows = (
+            jnp.sum(near_re * r_re - near_im * r_im, axis=0, keepdims=True),
+            jnp.sum(near_re * r_im + near_im * r_re, axis=0, keepdims=True),
+        )
+        found = tile[...]
+        for part in range(2):
+            for p in range(ops):
+                half = rows[part][:, p // 2 * width : (p // 2 + 1) * width]
+                keep = low_row if p % 2 == 0 else jnp.logical_not(low_row)
+                value = jnp.sum(jnp.where(keep, half, 0.0), axis=1, keepdims=True) / nev
+                spot = jnp.logical_and(row_id == part * ops + p, lane_id == t0)
+                found = jnp.where(spot, value, found)
+        tile[...] = found
+        return carry
+
+    lax.fori_loop(0, slices, step, 0)
+    gathered[me] = tile[...]
+    ends = [to_space(2, d, tile, gathered.at[me]) for d in range(1, spaces)]
+    for copy in ends:
+        copy.start()
+    for copy in shares + ends:
+        copy.wait_recv()
+    for copy in sums + fars + shares + ends:
+        copy.wait_send()
+
+
+def signed_roll_3d(ref):
+    block = ref[...].astype(jnp.float32)
+    half = block.shape[-1] // 2
+    turned = pltpu.roll(block, half, 2)
+    low = lax.broadcasted_iota(jnp.int32, block.shape, 2) < half
+    return jnp.where(low, -turned, turned).astype(jnp.bfloat16)
+
+
 def local(eigvecs, gauge_links, perambulators, momenta):
     spaces = lax.axis_size("space")
     z_total = spaces // YB
@@ -239,6 +390,38 @@
         compiler_params=pltpu.CompilerParams(vmem_limit_bytes=VMEM_LIMIT),
         name="smear",
     )(v, up, down, u, zlink, row_above, row_below, cos_all, sin_all)
+
+    slices = lax.axis_size("tm")
+    if op_count % (2 * spaces) == 0 and t_all == slices and pair_count % 2 == 0:
+        ops, width = op_count // spaces, 2 * nev
+        peers = max(spaces, slices)
+        every, gathered = pl.pallas_call(
+            functools.partial(exchange_kernel, spaces, slices),
+            out_shape=(
+                jax.ShapeDtypeStruct((op_count, nev, width), jnp.bfloat16),
+                jax.ShapeDtypeStruct((spaces, 2 * ops, width), jnp.float32),
+            ),
+            in_specs=[pl.BlockSpec(memory_space=pltpu.VMEM)] * 2,
+            out_specs=[pl.BlockSpec(memory_space=pltpu.VMEM)] * 2,
+            scratch_shapes=[
+                pltpu.VMEM((spaces, ops, nev, width), jnp.float32),
+                pltpu.VMEM((slices, ops, nev, width), jnp.bfloat16),
+                pltpu.VMEM((pair_count * nev, ops * width), jnp.bfloat16),
+                pltpu.VMEM((t_all, pair_count * nev, width), jnp.bfloat16),
+                pltpu.VMEM((ops * width, width), jnp.bfloat16),
+                pltpu.VMEM((2 * ops, width), jnp.float32),
+                pltpu.SemaphoreType.DMA((4, peers)),
+                pltpu.SemaphoreType.DMA((4, peers)),
+            ],
+            compiler_params=pltpu.CompilerParams(
+                collective_id=0, has_side_effects=True, vmem_limit_bytes=VMEM_LIMIT
+            ),
+            name="exchange",
+        )(partial_sums, both)
+        found = gathered[:, :, :t_all].reshape(spaces, 2, ops, t_all)
+        correlator = jnp.swapaxes(found, 0, 1).reshape(2, op_count, 1, t_all)
+        elementals = jnp.swapaxes(every.reshape(op_count, nev, 2, nev), 1, 2)[:, None]
+        return (smeared.reshape(eigvecs.shape), elementals, correlator)
 
     if op_count % spaces == 0:
         own = lax.psum_scatter(partial_sums, "space", scatter_dimension=0, tiled=True)

time: 189 us -> 79.8 us (0.42)
  waiting for transfers between devices: 75.7 us -> 7.15 us
  blocking collectives: 67.5 us -> 0 us
  Pallas kernels: 13.3 us -> 52.7 us
  between operations: 14.3 us -> 0.78 us
  other arithmetic: 3.76 us -> 7.02 us
  local copies, waits for them, and re-layouts: 6.78 us -> 4.86 us
    reduce_scatter x1 -> x0, waiting for transfers between devices: 71 us -> none  [local(): lax.psum_scatter(partial_sums, 'space', scatter_dimension=0, tiled=True)]
    all_gather x3 -> x0, blocking collectives: 67.5 us -> none  [the longest x1 31.4 us: local(): every = lax.all_gather(own, 'space', axis=0, tiled=True)]
    pallas_call x1, Pallas kernels: 5.44 us -> 44.8 us  [local(): pl.pallas_call(functools.partial(exchange_kernel, spaces, slices), out_sh...]
    unnamed x6, other arithmetic: 1.56 us -> 4.65 us
    ppermute x4, waiting for transfers between devices: 4.73 us -> 7.15 us  [along(): return lax.ppermute(value, 'space', pairs)]
    pallas_call x1 -> x0, local copies, waits for them, and re-layouts: 1.96 us -> none  [local(): pl.pallas_call(functools.partial(smear_kernel, 1.0 / math.sqrt(3.0 * z_to...]
  transfers between devices with their start and end apart: 5 -> 4, of which waited for: 2 -> 1; matrix products, arithmetic and copies ran while one was open for 1% -> 11% of each run, Pallas kernels for 0% -> 0%
where the time goes in v2:
time: 79.8 us; the launch traced here: 79.5 us
  Pallas kernels  52.7 us (66%)
  waiting for transfers between devices  7.15 us (9%)
  other arithmetic  7.02 us (9%)
  starting transfers between devices  7 us (9%)
  local copies, waits for them, and re-layouts  4.86 us (6%)
    pallas_call x1, Pallas kernels, local(): pl.pallas_call(functools.partial(exchange_kernel, spaces, slices), out_sh...  44.8 us
    pallas_call x1, Pallas kernels, local(): pl.pallas_call(functools.partial(smear_kernel, 1.0 / math.sqrt(3.0 * z_to...  7.89 us
    ppermute x4, waiting for transfers between devices, along(): return lax.ppermute(value, 'space', pairs)  7.15 us
    ppermute x4, starting transfers between devices, along(): return lax.ppermute(value, 'space', pairs)  7 us
    unnamed x6, other arithmetic  4.65 us
    reshape x2, local copies, waits for them, and re-layouts, local(): every.reshape(op_count, nev, 2, nev)  1.64 us
  transfers between devices with their start and end apart: 4, of which 1 were waited for; matrix products, arithmetic and copies ran while one was open for 11% of the time, Pallas kernels for 0%

profile of v2, /device:TPU:0, one launch (start us, length us, event | category | flops | bytes accessed | tf_op | source)
XLA Modules:
  0.0 79.5 jit_solution(16931645877681362165)
XLA Ops:
  0.6 0.0 copy-start.1
  0.6 0.0 copy-start
  0.7 0.9 %slice_reduce_fusion = f32[2,3,3,144]{3,2,1,0:T(4,128)S(1)} fusion(f32[3,1,2,3,3,1,144]{6,5,4,3,2,1,0:T(1,128)} %param.5), kind=kLoop, calls=%fused_computation.27 | loop fusion | bytes 20736 | tf_op jit(solution)/shard_map/slice | solution.py:363
  1.6 4.1 %collective-permute-start.1 = (f32[18,144]{1,0:T(8,128)S(1)}, f32[18,144]{1,0:T(8,128)S(1)}, u32[]{:S(2)}, u32[]{:S(2)}) collective-permute-start(f32[18,144]{1,0:T(8,128)S(1)} %squeeze.6), channel_id=1, source_target_pairs={{0,16},{4,20},{8,24},{12,28},{16,0},{20,4},{24,8},{28,12},{1,17},{... | collective-permute-start | bytes 31112 | tf_op jit(solution)/shard_map/ppermute | solution.py:358
  5.7 1.0 %copy.44 = f32[1,2,3,64,1,144]{5,3,4,2,1,0:T(8,128)S(1)} copy(f32[1,2,3,64,1,144]{5,4,3,2,1,0:T(1,128)} %param.4) | data formatting | bytes 442368
  6.7 0.7 bitcast_convert_fusion
  7.4 0.0 collective-permute-start
  7.5 2.9 %collective-permute-start.2 = (f32[6,64,24]{2,1,0:T(8,128)S(1)}, f32[6,64,24]{2,1,0:T(8,128)S(1)}, u32[]{:S(2)}, u32[]{:S(2)}) collective-permute-start(f32[6,64,24]{2,1,0:T(8,128)S(1)} %slice.141), channel_id=1, source_target_pairs={{0,12},{4,0},{8,4},{12,8},{16,28},{20,16},{24,20},{28,24},{1,13},{... | collective-permute-start | bytes 110600 | tf_op jit(solution)/shard_map/ppermute | solution.py:358
  10.3 1.0 %reduce = f32[3,2,3,3,144]{4,3,2,1,0:T(4,128)S(1)} reduce(f32[3,1,2,3,3,1,144]{6,5,4,3,2,1,0:T(1,128)} %param.5, f32[]{:T(128)} %constant.84), dimensions={1,5}, to_apply=%param.5.reduce_sub_computation | reduce | bytes 62212 | tf_op args[1]
  11.3 0.1 fusion.21
  11.4 0.7 add_dynamic-update-slice_fusion.5
  12.2 0.7 add_dynamic-update-slice_fusion.4
  12.9 0.7 add_dynamic-update-slice_fusion.3
  13.7 0.7 add_dynamic-update-slice_fusion.2
  14.4 0.7 add_dynamic-update-slice_fusion.1
  15.1 0.7 add_dynamic-update-slice_fusion
  15.9 0.0 collective-permute-start.3
  15.9 0.0 copy-done.1
  15.9 0.2 copy.39
  16.1 0.1 slice_bitcast_fusion.1
  16.3 0.2 sine_negate_fusion
  16.5 0.6 pad_maximum_fusion.bc
  17.1 0.0 collective-permute-done.1.zb
  17.1 0.0 collective-permute-done.2.ra
  17.1 7.1 %collective-permute-done.3.rb = f32[6,64,24]{2,1,0:T(8,128)S(1)} collective-permute-done((f32[6,64,24]{2,1,0:T(8,128)}, f32[6,64,24]{2,1,0:T(8,128)S(1)}, u32[]{:S(2)}, u32[]{:S(2)}) %collective-permute-start.3) | collective-permute-done | bytes 36896 | tf_op jit(solution)/shard_map/ppermute | solution.py:358
  24.3 0.0 collective-permute-done.up.down
  24.3 7.9 %smear.1 = (bf16[6,64,144]{2,1,0:T(8,128)(2,1)}, f32[32,64,128]{2,1,0:T(8,128)S(1)}) custom-call(f32[6,64,144]{2,1,0:T(8,128)S(1)} %bitcast.72, bf16[6,64,144]{2,1,0:T(8,128)(2,1)S(1)} %collective-permute-done.up.down, bf16[6,64,144]{2,1,0:T(8,128)(2,1)S(1)} %collective-permute-done.up.down, f32[3,18,144]{2,1,0:T(8,128)S(1)} %reshape.348.u, ...), custom_call_target="tpu_custom_call" | custom-call | tf_op jit(solution)/shard_map/smear/pallas_call | solution.py:378
  32.2 44.8 %exchange.1 = (bf16[32,64,128]{2,1,0:T(8,128)(2,1)S(1)}, f32[8,8,128]{2,1,0:T(8,128)S(1)}) custom-call(f32[32,64,128]{2,1,0:T(8,128)S(1)} %get-tuple-element.8.partial, bf16[4,1024,128]{2,1,0:T(8,128)(2,1)S(1)} %pad_maximum_fusion.bc), custom_call_target="tpu_custom_call" | custom-call | tf_op jit(solution)/shard_map/exchange/pallas_call | solution.py:398
  77.0 0.2 copy.41
  77.2 0.7 reshape.353
  77.9 0.4 reshape.351
  78.3 1.2 %copy.48 = bf16[32,64,2,64]{3,1,2,0:T(8,128)(2,1)} copy(bf16[32,64,2,64]{3,2,1,0:T(2,128)(2,1)S(1)} %reshape.351) | data formatting | bytes 1048576 | tf_op jit(solution)/shard_map/reshape | solution.py:423
  (7 shorter events, 0.1 us)
Async XLA Ops:
  0.6 15.2 %copy-start.1 = (s32[32,3]{0,1:T(4,128)S(1)}, s32[32,3]{0,1:T(4,128)}, u32[]{:S(2)}) copy-start(s32[32,3]{0,1:T(4,128)} %param.7) | copy-start | bytes 1156
  0.6 15.3 %copy-start = (bf16[1,4,2,4,4,64,64]{6,5,4,3,2,1,0:T(8,128)(2,1)S(1)}, bf16[1,4,2,4,4,64,64]{6,5,4,3,2,1,0:T(8,128)(2,1)}, u32[]{:S(2)}) copy-start(bf16[1,4,2,4,4,64,64]{6,5,4,3,2,1,0:T(8,128)(2,1)} %param.6) | copy-start | bytes 3145732
  1.6 15.5 %collective-permute-start.1 = (f32[18,144]{1,0:T(8,128)S(1)}, f32[18,144]{1,0:T(8,128)S(1)}, u32[]{:S(2)}, u32[]{:S(2)}) collective-permute-start(f32[18,144]{1,0:T(8,128)S(1)} %squeeze.6), channel_id=1, source_target_pairs={{0,16},{4,20},{8,24},{12,28},{16,0},{20,4},{24,8},{28,12},{1,17},{... | collective-permute-start | bytes 31112 | tf_op jit(solution)/shard_map/ppermute | solution.py:358
  7.4 16.8 %collective-permute-start = (bf16[6,64,144]{2,1,0:T(8,128)(2,1)}, bf16[6,64,144]{2,1,0:T(8,128)(2,1)S(1)}, u32[]{:S(2)}, u32[]{:S(2)}) collective-permute-start(bf16[6,64,144]{2,1,0:T(8,128)(2,1)} %bitcast_convert_fusion), channel_id=1, source_target_pairs={{0,16},{4,20},{8,24},{12,28},{16,0},{20,4},{24,8},{28,12},{1,17},{... | collective-permute-start | bytes 331784 | tf_op jit(solution)/shard_map/ppermute | solution.py:358
  7.5 9.6 %collective-permute-start.2 = (f32[6,64,24]{2,1,0:T(8,128)S(1)}, f32[6,64,24]{2,1,0:T(8,128)S(1)}, u32[]{:S(2)}, u32[]{:S(2)}) collective-permute-start(f32[6,64,24]{2,1,0:T(8,128)S(1)} %slice.141), channel_id=1, source_target_pairs={{0,12},{4,0},{8,4},{12,8},{16,28},{20,16},{24,20},{28,24},{1,13},{... | collective-permute-start | bytes 110600 | tf_op jit(solution)/shard_map/ppermute | solution.py:358
  15.9 8.4 %collective-permute-start.3 = (f32[6,64,24]{2,1,0:T(8,128)}, f32[6,64,24]{2,1,0:T(8,128)S(1)}, u32[]{:S(2)}, u32[]{:S(2)}) collective-permute-start(f32[6,64,24]{2,1,0:T(8,128)} %add_dynamic-update-slice_fusion), channel_id=1, source_target_pairs={{0,4},{4,8},{8,12},{12,0},{16,20},{20,24},{24,28},{28,16},{1,5},{5... | collective-permute-start | bytes 110600 | tf_op jit(solution)/shard_map/ppermute | solution.py:358

commit v3 on v2

--- a/solution.py
+++ b/solution.py
@@ -124,6 +124,11 @@
         sm[i] = rounded
         wide[i] = rounded.astype(jnp.float32)
 
+    form_elementals(norm_scale, cs, sn, sm, wide, elem)
+
+
+def form_elementals(norm_scale, cs, sn, sm, wide, elem):
+    nev = wide.shape[1]
     per = 2 if elem.shape[0] % 2 == 0 else 1
 
     def step(g, carry):
@@ -149,6 +154,122 @@
     lax.fori_loop(0, elem.shape[0] // per, step, 0)
 
 
+def halo_smear_kernel(
+    norm_scale, v, u, cs, sn, sm, elem, pad, wide, prod, sums, narrow, other, zb, edge, got, send, recv
+):
+    me, mine = lax.axis_index("space"), lax.axis_index("tm")
+    spaces = lax.axis_size("space")
+    nev, sites = v.shape[1], v.shape[2]
+    lanes = pad.shape[2]
+    z, y = me // YB, me % YB
+    across = (me + YB) % spaces
+    above = z * YB + (y + 1) % YB
+    below = z * YB + (y + YB - 1) % YB
+    barrier = pltpu.get_barrier_semaphore()
+    for device in (across, above, below):
+        pl.semaphore_signal(
+            barrier, inc=1, device_id=(device, mine), device_id_type=pl.DeviceIdType.MESH
+        )
+
+    def remote(k, source, target, device):
+        return pltpu.make_async_remote_copy(
+            src_ref=source,
+            dst_ref=target,
+            send_sem=send.at[k],
+            recv_sem=recv.at[k],
+            device_id=(device, mine),
+            device_id_type=pl.DeviceIdType.MESH,
+        )
+
+    for i in range(6):
+        narrow[i] = v[i].astype(jnp.bfloat16)
+    pl.semaphore_wait(barrier, 3)
+    copies = [
+        remote(0, narrow, other, across),
+        remote(1, u.at[2], zb, across),
+        remote(2, edge.at[0], got.at[0], below),
+        remote(3, edge.at[1], got.at[1], above),
+    ]
+    copies[0].start()
+    copies[1].start()
+    lane = lax.broadcasted_iota(jnp.int32, (nev, lanes), 1)
+    x_coord = lane % LX
+    last = sites - LX
+    pad[...] = jnp.zeros_like(pad)
+    prod[...] = jnp.zeros_like(prod)
+    for i in range(6):
+        pad[i, :, :sites] = v[i]
+        sums[i] = (1.0 - 6.0 * KAPPA) * v[i]
+
+    def add(terms):
+        for i in range(6):
+            sums[i] = sums[i] + KAPPA * terms[i]
+
+    def link(d):
+        return lambda k: u[d, k : k + 1, :]
+
+    for i, term in enumerate(link_times(link(1), lambda i: v[i], True)):
+        prod[i, :, :sites] = term
+    for side, (ref, start) in enumerate(((pad, 0), (prod, last))):
+        packed = jnp.zeros((nev, lanes), jnp.float32)
+        for i in range(6):
+            inside = jnp.logical_and(lane >= i * LX, lane < (i + 1) * LX)
+            packed = jnp.where(
+                inside, pltpu.roll(ref[i], (i * LX - start + lanes) % lanes, 1), packed
+            )
+        edge[side] = packed
+    copies[2].start()
+    copies[3].start()
+
+    def forward_x(i):
+        return jnp.where(
+            x_coord == LX - 1, pltpu.roll(pad[i], LX - 1, 1), pltpu.roll(pad[i], lanes - 1, 1)
+        )[:, :sites]
+
+    def forward_y(i):
+        return jnp.where(
+            lane >= last,
+            pltpu.roll(got[0], (last - i * LX + lanes) % lanes, 1),
+            pltpu.roll(pad[i], lanes - LX, 1),
+        )[:, :sites]
+
+    def behind_y(i):
+        return jnp.where(
+            lane < LX,
+            pltpu.roll(got[1], (lanes - i * LX) % lanes, 1),
+            pltpu.roll(prod[i], LX, 1),
+        )[:, :sites]
+
+    add(link_times(link(0), forward_x, False))
+    for i, term in enumerate(link_times(link(0), lambda i: v[i], True)):
+        wide[i] = term
+    copies[2].wait_recv()
+    copies[3].wait_recv()
+    add(link_times(link(1), forward_y, False))
+    add([behind_y(i) for i in range(6)])
+    for i in range(6):
+        prod[i, :, :sites] = wide[i]
+    add(
+        [
+            jnp.where(
+                x_coord == 0, pltpu.roll(prod[i], lanes - LX + 1, 1), pltpu.roll(prod[i], 1, 1)
+            )[:, :sites]
+            for i in range(6)
+        ]
+    )
+    copies[0].wait_recv()
+    copies[1].wait_recv()
+    add(link_times(link(2), lambda i: other[i].astype(jnp.float32), False))
+    add(link_times(lambda k: zb[k : k + 1, :], lambda i: other[i].astype(jnp.float32), True))
+    for i in range(6):
+        rounded = sums[i].astype(jnp.bfloat16)
+        sm[i] = rounded
+        wide[i] = rounded.astype(jnp.float32)
+    form_elementals(norm_scale, cs, sn, sm, wide, elem)
+    for copy in copies:
+        copy.wait_send()
+
+
 def trace_kernel(far, bc, g_re, g_im, out, left, b2, weights):
     ops = far.shape[1]
     nev, width = far.shape[2], far.shape[3]
@@ -189,7 +310,7 @@
 
 
 def exchange_kernel(
-    spaces, slices, partial, bc, every, gathered, inbox, far, left, b2, weights, tile, send, recv
+    spaces, slices, partial, bc, every, gathered, inbox, middle, far, left, b2, weights, tile, send, recv
 ):
     me, mine = lax.axis_index("space"), lax.axis_index("tm")
     ops, nev, width = inbox.shape[1:]
@@ -206,48 +327,64 @@
         )
     pl.semaphore_wait(barrier, spaces + slices - 2)
 
-    def to_space(kind, d, source, target):
+    depth, side, level = spaces // 2, me % 2, me // 2
+    partner = me + 1 - 2 * side
+
+    def remote(kind, d, source, target, device):
         return pltpu.make_async_remote_copy(
             src_ref=source,
             dst_ref=target,
             send_sem=send.at[kind, d],
             recv_sem=recv.at[kind, d],
-            device_id=((me + d) % spaces, mine),
+            device_id=device,
             device_id_type=pl.DeviceIdType.MESH,
         )
 
-    def to_slice(d, source, target):
-        return pltpu.make_async_remote_copy(
-            src_ref=source,
-            dst_ref=target,
-            send_sem=send.at[3, d],
-            recv_sem=recv.at[3, d],
-            device_id=(me, (mine + d) % slices),
-            device_id_type=pl.DeviceIdType.MESH,
-        )
-
-    sums = [
-        to_space(0, d, partial.at[pl.ds((me + d) % spaces * ops, ops)], inbox.at[d])
-        for d in range(1, spaces)
-    ]
-    for copy in sums:
-        copy.start()
+    def block_of(ref, device):
+        return ref.at[pl.ds(device * ops, ops)]
+
+    order = list(range(depth - 1, -1, -1))
+    beside = {}
+    for d in order:
+        there = (level + d) % depth * 2
+        beside[d] = remote(
+            0, d, block_of(partial, there + 1 - side), inbox.at[d], (partner, mine)
+        )
+        beside[d].start()
     b2[...] = signed_roll_3d(bc)
-    total = partial[pl.ds(me * ops, ops)]
-    for d, copy in enumerate(sums, 1):
-        copy.wait_recv()
-        total = total + inbox[d]
+    along = {}
+    for d in order:
+        beside[d].wait_recv()
+        there = (level + d) % depth * 2
+        total = partial[pl.ds((there + side) * ops, ops)] + inbox[d]
+        if d > 0:
+            middle[d] = total
+            along[d] = remote(1, d, middle.at[d], inbox.at[depth + d], (there + side, mine))
+            along[d].start()
+    for d in order[:-1]:
+        along[d].wait_recv()
+        total = total + inbox[depth + d]
     rounded = total.astype(jnp.bfloat16)
     far[mine] = rounded
     every[pl.ds(me * ops, ops)] = rounded
-    fars = [to_slice(d, far.at[mine], far.at[mine]) for d in range(1, slices)]
-    for copy in fars:
-        copy.start()
-    shares = [
-        to_space(1, d, far.at[mine], every.at[pl.ds(me * ops, ops)]) for d in range(1, spaces)
-    ]
-    for copy in shares:
-        copy.start()
+
+    def far_copy(d):
+        return remote(3, d, far.at[mine], far.at[mine], (me, (mine + d) % slices))
+
+    def share_copy(d):
+        there = (level + d) % depth * 2 + side
+        return remote(4, d, far.at[mine], block_of(every, me), (there, mine))
+
+    def pass_copy(d):
+        origin = (level + depth - d) % depth * 2 + side
+        return remote(5, d, block_of(every, origin), block_of(every, origin), (partner, mine))
+
+    for d in range(1, slices):
+        far_copy(d).start()
+    for d in range(1, depth):
+        share_copy(d).start()
+    own_pass = remote(5, 0, far.at[mine], block_of(every, me), (partner, mine))
+    own_pass.start()
 
     near = rounded.astype(jnp.float32)
     low = lax.broadcasted_iota(jnp.int32, (nev, width), 1) < nev
@@ -266,14 +403,12 @@
     def step(d, carry):
         @pl.when(d > 0)
         def _():
-            pltpu.make_async_remote_copy(
-                src_ref=far.at[mine],
-                dst_ref=far.at[mine],
-                send_sem=send.at[3, d],
-                recv_sem=recv.at[3, d],
-                device_id=(me, (mine + d) % slices),
-                device_id_type=pl.DeviceIdType.MESH,
-            ).wait_recv()
+            far_copy(d).wait_recv()
+
+        @pl.when(jnp.logical_and(d > 0, d < depth))
+        def _():
+            share_copy(d).wait_recv()
+            pass_copy(d).start()
 
         t0 = (mine + slices - d) % slices
         for p in range(ops):
@@ -322,12 +457,17 @@
 
     lax.fori_loop(0, slices, step, 0)
     gathered[me] = tile[...]
-    ends = [to_space(2, d, tile, gathered.at[me]) for d in range(1, spaces)]
+    ends = [
+        remote(2, d, tile, gathered.at[me], ((me + d) % spaces, mine)) for d in range(1, spaces)
+    ]
     for copy in ends:
         copy.start()
-    for copy in shares + ends:
+    passes = [own_pass] + [pass_copy(d) for d in range(1, depth)]
+    for copy in passes + ends:
         copy.wait_recv()
-    for copy in sums + fars + shares + ends:
+    shares = [share_copy(d) for d in range(1, depth)]
+    fars = [far_copy(d) for d in range(1, slices)]
+    for copy in list(beside.values()) + list(along.values()) + fars + shares + passes + ends:
         copy.wait_send()
 
 
@@ -357,17 +497,6 @@
             pairs.append((s, (z + z_steps) % z_total * YB + (y + y_steps) % YB))
         return lax.ppermute(value, "space", pairs)
 
-    narrow = v.astype(jnp.bfloat16)
-    up = along(narrow, -1, 0)
-    down = up if z_total == 2 else along(narrow, 1, 0)
-    zlink = along(u[2], 1, 0)
-    edge = jnp.stack(
-        link_times(
-            lambda k: u[1, k : k + 1, sites - LX :], lambda i: v[i, :, sites - LX :], True
-        )
-    )
-    row_above = along(v[:, :, :LX], 0, -1)
-    row_below = along(edge, 0, 1)
     cos_all, sin_all = phases(momenta, z_index, y_block * (sites // LX), sites, z_total)
     t_all = perambulators.shape[1]
     pair_count = perambulators.shape[3] * perambulators.shape[4]
@@ -375,24 +504,64 @@
     both = jnp.concatenate([blocks[:, 0], blocks[:, 1]], axis=2)
 
     lanes = -(-sites // 128) * 128
-    smeared, partial_sums = pl.pallas_call(
-        functools.partial(smear_kernel, 1.0 / math.sqrt(3.0 * z_total * LX * LX)),
-        out_shape=(
-            jax.ShapeDtypeStruct((6, nev, sites), jnp.bfloat16),
-            jax.ShapeDtypeStruct((op_count, nev, 2 * nev), jnp.float32),
-        ),
-        scratch_shapes=[
-            pltpu.VMEM((6, nev, lanes), jnp.float32),
-            pltpu.VMEM((6, nev, sites), jnp.float32),
-            pltpu.VMEM((6, nev, lanes), jnp.float32),
-            pltpu.VMEM((6, nev, sites), jnp.float32),
-        ],
-        compiler_params=pltpu.CompilerParams(vmem_limit_bytes=VMEM_LIMIT),
-        name="smear",
-    )(v, up, down, u, zlink, row_above, row_below, cos_all, sin_all)
+    norm_scale = 1.0 / math.sqrt(3.0 * z_total * LX * LX)
+    if z_total == 2 and lanes >= 6 * LX:
+        smeared, partial_sums = pl.pallas_call(
+            functools.partial(halo_smear_kernel, norm_scale),
+            out_shape=(
+                jax.ShapeDtypeStruct((6, nev, sites), jnp.bfloat16),
+                jax.ShapeDtypeStruct((op_count, nev, 2 * nev), jnp.float32),
+            ),
+            in_specs=[pl.BlockSpec(memory_space=pltpu.VMEM)] * 4,
+            out_specs=[pl.BlockSpec(memory_space=pltpu.VMEM)] * 2,
+            scratch_shapes=[
+                pltpu.VMEM((6, nev, lanes), jnp.float32),
+                pltpu.VMEM((6, nev, sites), jnp.float32),
+                pltpu.VMEM((6, nev, lanes), jnp.float32),
+                pltpu.VMEM((6, nev, sites), jnp.float32),
+                pltpu.VMEM((6, nev, sites), jnp.bfloat16),
+                pltpu.VMEM((6, nev, sites), jnp.bfloat16),
+                pltpu.VMEM((18, sites), jnp.float32),
+                pltpu.VMEM((2, nev, lanes), jnp.float32),
+                pltpu.VMEM((2, nev, lanes), jnp.float32),
+                pltpu.SemaphoreType.DMA((4,)),
+                pltpu.SemaphoreType.DMA((4,)),
+            ],
+            compiler_params=pltpu.CompilerParams(
+                collective_id=1, has_side_effects=True, vmem_limit_bytes=VMEM_LIMIT
+            ),
+            name="halo_smear",
+        )(v, u, cos_all, sin_all)
+    else:
+        narrow = v.astype(jnp.bfloat16)
+        up = along(narrow, -1, 0)
+        down = up if z_total == 2 else along(narrow, 1, 0)
+        zlink = along(u[2], 1, 0)
+        edge = jnp.stack(
+            link_times(
+                lambda k: u[1, k : k + 1, sites - LX :], lambda i: v[i, :, sites - LX :], True
+            )
+        )
+        row_above = along(v[:, :, :LX], 0, -1)
+        row_below = along(edge, 0, 1)
+        smeared, partial_sums = pl.pallas_call(
+            functools.partial(smear_kernel, 1.0 / math.sqrt(3.0 * z_total * LX * LX)),
+            out_shape=(
+                jax.ShapeDtypeStruct((6, nev, sites), jnp.bfloat16),
+                jax.ShapeDtypeStruct((op_count, nev, 2 * nev), jnp.float32),
+            ),
+            scratch_shapes=[
+                pltpu.VMEM((6, nev, lanes), jnp.float32),
+                pltpu.VMEM((6, nev, sites), jnp.float32),
+                pltpu.VMEM((6, nev, lanes), jnp.float32),
+                pltpu.VMEM((6, nev, sites), jnp.float32),
+            ],
+            compiler_params=pltpu.CompilerParams(vmem_limit_bytes=VMEM_LIMIT),
+            name="smear",
+        )(v, up, down, u, zlink, row_above, row_below, cos_all, sin_all)
 
     slices = lax.axis_size("tm")
-    if op_count % (2 * spaces) == 0 and t_all == slices and pair_count % 2 == 0:
+    if op_count % (2 * spaces) == 0 and t_all == slices and pair_count % 2 == 0 and spaces <= 2 * slices:
         ops, width = op_count // spaces, 2 * nev
         peers = max(spaces, slices)
         every, gathered = pl.pallas_call(
@@ -405,13 +574,14 @@
             out_specs=[pl.BlockSpec(memory_space=pltpu.VMEM)] * 2,
             scratch_shapes=[
                 pltpu.VMEM((spaces, ops, nev, width), jnp.float32),
+                pltpu.VMEM((spaces // 2, ops, nev, width), jnp.float32),
                 pltpu.VMEM((slices, ops, nev, width), jnp.bfloat16),
                 pltpu.VMEM((pair_count * nev, ops * width), jnp.bfloat16),
                 pltpu.VMEM((t_all, pair_count * nev, width), jnp.bfloat16),
                 pltpu.VMEM((ops * width, width), jnp.bfloat16),
                 pltpu.VMEM((2 * ops, width), jnp.float32),
-                pltpu.SemaphoreType.DMA((4, peers)),
-                pltpu.SemaphoreType.DMA((4, peers)),
+                pltpu.SemaphoreType.DMA((6, peers)),
+                pltpu.SemaphoreType.DMA((6, peers)),
             ],
             compiler_params=pltpu.CompilerParams(
                 collective_id=0, has_side_effects=True, vmem_limit_bytes=VMEM_LIMIT

time: 79.8 us -> 67.5 us (0.85)
  waiting for transfers between devices: 7.15 us -> 0 us
  starting transfers between devices: 7 us -> 0 us
  other arithmetic: 7.02 us -> 2.49 us
  Pallas kernels: 52.7 us -> 57 us
  local copies, waits for them, and re-layouts: 4.86 us -> 7.01 us
    pallas_call x1, Pallas kernels: 7.89 us -> 23 us  [local(): pl.pallas_call(functools.partial(halo_smear_kernel, norm_scale), out_shap...]
    pallas_call x1, Pallas kernels: 44.8 us -> 33.9 us  [local(): pl.pallas_call(functools.partial(exchange_kernel, spaces, slices), out_sh...]
    ppermute x4 -> x0, waiting for transfers between devices: 7.15 us -> none  [along(): return lax.ppermute(value, 'space', pairs)]
    ppermute x4 -> x0, starting transfers between devices: 7 us -> none  [along(): return lax.ppermute(value, 'space', pairs)]
    unnamed x6 -> x1, other arithmetic: 4.65 us -> 0.97 us
    unnamed x6 -> x3, local copies, waits for them, and re-layouts: 1.2 us -> 3.56 us
    slice x2 -> x0, local copies, waits for them, and re-layouts: 0.94 us -> none  [the longest x1 0.93 us: local(): zlink = along(u[2], 1, 0)]
  transfers between devices with their start and end apart: 4 -> 0, of which waited for: 1 -> 0; matrix products, arithmetic and copies ran while one was open for 11% -> 0% of each run, Pallas kernels for 0% -> 0%
where the time goes in v3:
time: 67.5 us; the launch traced here: 67.2 us
  Pallas kernels  57 us (84%)
  local copies, waits for them, and re-layouts  7.01 us (10%)
  other arithmetic  2.49 us (4%)
  between operations  0.73 us (1%)
    pallas_call x1, Pallas kernels, local(): pl.pallas_call(functools.partial(exchange_kernel, spaces, slices), out_sh...  33.9 us
    pallas_call x1, Pallas kernels, local(): pl.pallas_call(functools.partial(halo_smear_kernel, norm_scale), out_shap...  23 us
    unnamed x3, local copies, waits for them, and re-layouts  3.56 us
    reshape x2, local copies, waits for them, and re-layouts, local(): every.reshape(op_count, nev, 2, nev)  1.64 us

profile of v3, /device:TPU:0, one launch (start us, length us, event | category | flops | bytes accessed | tf_op | source)
XLA Modules:
  0.0 67.2 jit_solution(10354197299921953046)
XLA Ops:
  0.7 0.7 %fusion.17 = f32[32]{0:T(128)S(1)} fusion(s32[32,3]{0,1:T(4,128)} %param.7, s32[]{:T(128)S(6)} %select_n.51), kind=kLoop, calls=%fused_computation.34 | loop fusion | flops 448 | bytes 260 | tf_op jit(solution)/shard_map/add | solution.py:29
  1.3 0.8 %slice_bitcast_fusion.3 = (s32[32]{0:T(128)S(1)}, s32[32]{0:T(128)S(1)}) fusion(s32[32,3]{0,1:T(4,128)} %param.7), kind=kLoop, calls=%fused_computation.37 | loop fusion | bytes 512 | tf_op jit(solution)/shard_map/mul | solution.py:22
  2.1 0.2 sine_negate_fusion
  2.4 1.0 %reduce = f32[3,2,3,3,144]{4,3,2,1,0:T(4,128)S(1)} reduce(f32[3,1,2,3,3,1,144]{6,5,4,3,2,1,0:T(1,128)} %param.5, f32[]{:T(128)} %constant.84), dimensions={1,5}, to_apply=%param.5.reduce_sub_computation | reduce | bytes 62212 | tf_op args[1]
  3.4 1.0 %copy.16 = f32[1,2,3,64,1,144]{5,3,4,2,1,0:T(8,128)S(1)} copy(f32[1,2,3,64,1,144]{5,4,3,2,1,0:T(1,128)} %param.4) | data formatting | bytes 442368
  4.4 23.0 %halo_smear.1 = (bf16[6,64,144]{2,1,0:T(8,128)(2,1)S(1)}, f32[32,64,128]{2,1,0:T(8,128)S(1)}) custom-call(f32[6,64,144]{2,1,0:T(8,128)S(1)} %bitcast.28, f32[3,18,144]{2,1,0:T(8,128)S(1)} %reshape.49.u, f32[32,144]{1,0:T(8,128)S(1)} %get-tuple-element.20.cs, f32[32,144]{1,0:T(8,128)S(1)} %get-tuple-element.19.sn), custom_call_target="tpu_custom_call" | custom-call | tf_op jit(solution)/shard_map/halo_smear/pallas_call | solution.py:509
  27.4 1.9 %copy.11 = bf16[1,4,2,4,4,64,64]{6,5,4,3,1,2,0:T(8,128)(2,1)S(1)} copy(bf16[1,4,2,4,4,64,64]{6,5,4,3,2,1,0:T(8,128)(2,1)} %param.6) | data formatting | bytes 2097152 | tf_op args[2]
  29.3 0.1 slice_bitcast_fusion.1
  29.5 0.6 pad_maximum_fusion.bc
  30.0 33.9 %exchange.1 = (bf16[32,64,128]{2,1,0:T(8,128)(2,1)S(1)}, f32[8,8,128]{2,1,0:T(8,128)S(1)}) custom-call(f32[32,64,128]{2,1,0:T(8,128)S(1)} %get-tuple-element.8.partial, bf16[4,1024,128]{2,1,0:T(8,128)(2,1)S(1)} %pad_maximum_fusion.bc), custom_call_target="tpu_custom_call" | custom-call | tf_op jit(solution)/shard_map/exchange/pallas_call | solution.py:567
  64.0 0.2 copy.13
  64.2 0.7 %reshape.54 = f32[2,32,1,4]{1,3,0,2:T(4,128)} reshape(f32[2,8,4,4]{2,1,3,0:T(8,128)S(1)} %bitcast.33) | data formatting | bytes 2048 | tf_op jit(solution)/shard_map/reshape | solution.py:592
  64.9 0.4 reshape.52
  65.3 1.2 %copy.19 = bf16[32,64,2,64]{3,1,2,0:T(8,128)(2,1)} copy(bf16[32,64,2,64]{3,2,1,0:T(2,128)(2,1)S(1)} %reshape.52) | data formatting | bytes 1048576 | tf_op jit(solution)/shard_map/reshape | solution.py:593
  66.5 0.7 %copy.21 = bf16[1,2,3,64,1,144]{5,3,4,2,1,0:T(8,128)(2,1)} copy(bf16[1,2,3,64,1,144]{5,3,4,2,1,0:T(8,128)(2,1)S(1)} %bitcast.29) | data formatting | bytes 221184
  (2 shorter events, 0.0 us)

commit v4 on v3

--- a/solution.py
+++ b/solution.py
@@ -124,21 +124,22 @@
         sm[i] = rounded
         wide[i] = rounded.astype(jnp.float32)
 
-    form_elementals(norm_scale, cs, sn, sm, wide, elem)
-
-
-def form_elementals(norm_scale, cs, sn, sm, wide, elem):
+    form_elementals(norm_scale, cs, sn, sm, wide, elem, 0, elem.shape[0])
+
+
+def form_elementals(norm_scale, cs, sn, sm, wide, elem, first, count):
     nev = wide.shape[1]
-    per = 2 if elem.shape[0] % 2 == 0 else 1
-
-    def step(g, carry):
+    per = 2 if count % 2 == 0 else 1
+
+    def step(k, carry):
+        start = first + k * per
         product = None
         for colour in range(3):
             s_re, s_im = wide[colour], wide[3 + colour]
             parts = []
             for j in range(per):
-                cos_row = cs[pl.ds(g * per + j, 1), :]
-                sin_row = sn[pl.ds(g * per + j, 1), :]
+                cos_row = cs[pl.ds(start + j, 1), :]
+                sin_row = sn[pl.ds(start + j, 1), :]
                 parts.append((s_re * cos_row - s_im * sin_row).astype(jnp.bfloat16))
                 parts.append((s_re * sin_row + s_im * cos_row).astype(jnp.bfloat16))
             left = jnp.concatenate([sm[colour], sm[3 + colour]], axis=0)
@@ -148,17 +149,39 @@
             product = term if product is None else product + term
         for j in range(per):
             block = product[:, j * 2 * nev : (j + 1) * 2 * nev]
-            elem[g * per + j] = norm_scale * (block[:nev] + signed_roll(block[nev:], 1.0))
+            elem[start + j] = norm_scale * (block[:nev] + signed_roll(block[nev:], 1.0))
         return carry
 
-    lax.fori_loop(0, elem.shape[0] // per, step, 0)
-
-
-def halo_smear_kernel(
-    norm_scale, v, u, cs, sn, sm, elem, pad, wide, prod, sums, narrow, other, zb, edge, got, send, recv
+    lax.fori_loop(0, count // per, step, 0)
+
+
+def whole_kernel(
+    spaces,
+    slices,
+    norm_scale,
+    v,
+    u,
+    cs,
+    sn,
+    bc,
+    sm,
+    every,
+    gathered,
+    pad,
+    wide,
+    prod,
+    sums,
+    narrow,
+    other,
+    zb,
+    edge,
+    got,
+    send,
+    recv,
+    elem,
+    *rest,
 ):
     me, mine = lax.axis_index("space"), lax.axis_index("tm")
-    spaces = lax.axis_size("space")
     nev, sites = v.shape[1], v.shape[2]
     lanes = pad.shape[2]
     z, y = me // YB, me % YB
@@ -166,9 +189,13 @@
     above = z * YB + (y + 1) % YB
     below = z * YB + (y + YB - 1) % YB
     barrier = pltpu.get_barrier_semaphore()
-    for device in (across, above, below):
+    for d in range(1, spaces):
         pl.semaphore_signal(
-            barrier, inc=1, device_id=(device, mine), device_id_type=pl.DeviceIdType.MESH
+            barrier, inc=1, device_id=((me + d) % spaces, mine), device_id_type=pl.DeviceIdType.MESH
+        )
+    for d in range(1, slices):
+        pl.semaphore_signal(
+            barrier, inc=1, device_id=(me, (mine + d) % slices), device_id_type=pl.DeviceIdType.MESH
         )
 
     def remote(k, source, target, device):
@@ -183,7 +210,7 @@
 
     for i in range(6):
         narrow[i] = v[i].astype(jnp.bfloat16)
-    pl.semaphore_wait(barrier, 3)
+    pl.semaphore_wait(barrier, spaces + slices - 2)
     copies = [
         remote(0, narrow, other, across),
         remote(1, u.at[2], zb, across),
@@ -265,7 +292,13 @@
         rounded = sums[i].astype(jnp.bfloat16)
         sm[i] = rounded
         wide[i] = rounded.astype(jnp.float32)
-    form_elementals(norm_scale, cs, sn, sm, wide, elem)
+
+    ops = elem.shape[0] // spaces
+
+    def form(device):
+        form_elementals(norm_scale, cs, sn, sm, wide, elem, device * ops, ops)
+
+    exchange(form, spaces, slices, elem, bc, every, gathered, *rest)
     for copy in copies:
         copy.wait_send()
 
@@ -309,23 +342,12 @@
             out[0, part * ops + p : part * ops + p + 1, :] = jnp.broadcast_to(total, (1, width))
 
 
-def exchange_kernel(
-    spaces, slices, partial, bc, every, gathered, inbox, middle, far, left, b2, weights, tile, send, recv
+def exchange(
+    form, spaces, slices, partial, bc, every, gathered, inbox, middle, far, left, b2, weights, tile, send, recv
 ):
     me, mine = lax.axis_index("space"), lax.axis_index("tm")
     ops, nev, width = inbox.shape[1:]
     pairs = bc.shape[1] // nev
-
-    barrier = pltpu.get_barrier_semaphore()
-    for d in range(1, spaces):
-        pl.semaphore_signal(
-            barrier, inc=1, device_id=((me + d) % spaces, mine), device_id_type=pl.DeviceIdType.MESH
-        )
-    for d in range(1, slices):
-        pl.semaphore_signal(
-            barrier, inc=1, device_id=(me, (mine + d) % slices), device_id_type=pl.DeviceIdType.MESH
-        )
-    pl.semaphore_wait(barrier, spaces + slices - 2)
 
     depth, side, level = spaces // 2, me % 2, me // 2
     partner = me + 1 - 2 * side
@@ -344,16 +366,9 @@
         return ref.at[pl.ds(device * ops, ops)]
 
     order = list(range(depth - 1, -1, -1))
-    beside = {}
-    for d in order:
-        there = (level + d) % depth * 2
-        beside[d] = remote(
-            0, d, block_of(partial, there + 1 - side), inbox.at[d], (partner, mine)
-        )
-        beside[d].start()
-    b2[...] = signed_roll_3d(bc)
-    along = {}
-    for d in order:
+    beside, along = {}, {}
+
+    def hand_on(d):
         beside[d].wait_recv()
         there = (level + d) % depth * 2
         total = partial[pl.ds((there + side) * ops, ops)] + inbox[d]
@@ -361,6 +376,20 @@
             middle[d] = total
             along[d] = remote(1, d, middle.at[d], inbox.at[depth + d], (there + side, mine))
             along[d].start()
+        return total
+
+    for k, d in enumerate(order):
+        there = (level + d) % depth * 2
+        form(there + 1 - side)
+        beside[d] = remote(
+            0, d, block_of(partial, there + 1 - side), inbox.at[d], (partner, mine)
+        )
+        beside[d].start()
+        form(there + side)
+        if k > 0:
+            hand_on(order[k - 1])
+    b2[...] = signed_roll_3d(bc)
+    total = hand_on(0)
     for d in order[:-1]:
         along[d].wait_recv()
         total = total + inbox[depth + d]
@@ -505,15 +534,26 @@
 
     lanes = -(-sites // 128) * 128
     norm_scale = 1.0 / math.sqrt(3.0 * z_total * LX * LX)
-    if z_total == 2 and lanes >= 6 * LX:
-        smeared, partial_sums = pl.pallas_call(
-            functools.partial(halo_smear_kernel, norm_scale),
+    slices = lax.axis_size("tm")
+    if (
+        z_total == 2
+        and lanes >= 6 * LX
+        and op_count % (2 * spaces) == 0
+        and t_all == slices
+        and pair_count % 2 == 0
+        and spaces <= 2 * slices
+    ):
+        ops, width = op_count // spaces, 2 * nev
+        peers = max(spaces, slices)
+        smeared, every, gathered = pl.pallas_call(
+            functools.partial(whole_kernel, spaces, slices, norm_scale),
             out_shape=(
                 jax.ShapeDtypeStruct((6, nev, sites), jnp.bfloat16),
-                jax.ShapeDtypeStruct((op_count, nev, 2 * nev), jnp.float32),
+                jax.ShapeDtypeStruct((op_count, nev, width), jnp.bfloat16),
+                jax.ShapeDtypeStruct((spaces, 2 * ops, width), jnp.float32),
             ),
-            in_specs=[pl.BlockSpec(memory_space=pltpu.VMEM)] * 4,
-            out_specs=[pl.BlockSpec(memory_space=pltpu.VMEM)] * 2,
+            in_specs=[pl.BlockSpec(memory_space=pltpu.VMEM)] * 5,
+            out_specs=[pl.BlockSpec(memory_space=pltpu.VMEM)] * 3,
             scratch_shapes=[
                 pltpu.VMEM((6, nev, lanes), jnp.float32),
                 pltpu.VMEM((6, nev, sites), jnp.float32),
@@ -526,53 +566,7 @@
                 pltpu.VMEM((2, nev, lanes), jnp.float32),
                 pltpu.SemaphoreType.DMA((4,)),
                 pltpu.SemaphoreType.DMA((4,)),
-            ],
-            compiler_params=pltpu.CompilerParams(
-                collective_id=1, has_side_effects=True, vmem_limit_bytes=VMEM_LIMIT
-            ),
-            name="halo_smear",
-        )(v, u, cos_all, sin_all)
-    else:
-        narrow = v.astype(jnp.bfloat16)
-        up = along(narrow, -1, 0)
-        down = up if z_total == 2 else along(narrow, 1, 0)
-        zlink = along(u[2], 1, 0)
-        edge = jnp.stack(
-            link_times(
-                lambda k: u[1, k : k + 1, sites - LX :], lambda i: v[i, :, sites - LX :], True
-            )
-        )
-        row_above = along(v[:, :, :LX], 0, -1)
-        row_below = along(edge, 0, 1)
-        smeared, partial_sums = pl.pallas_call(
-            functools.partial(smear_kernel, 1.0 / math.sqrt(3.0 * z_total * LX * LX)),
-            out_shape=(
-                jax.ShapeDtypeStruct((6, nev, sites), jnp.bfloat16),
-                jax.ShapeDtypeStruct((op_count, nev, 2 * nev), jnp.float32),
-            ),
-            scratch_shapes=[
-                pltpu.VMEM((6, nev, lanes), jnp.float32),
-                pltpu.VMEM((6, nev, sites), jnp.float32),
-                pltpu.VMEM((6, nev, lanes), jnp.float32),
-                pltpu.VMEM((6, nev, sites), jnp.float32),
-            ],
-            compiler_params=pltpu.CompilerParams(vmem_limit_bytes=VMEM_LIMIT),
-            name="smear",
-        )(v, up, down, u, zlink, row_above, row_below, cos_all, sin_all)
-
-    slices = lax.axis_size("tm")
-    if op_count % (2 * spaces) == 0 and t_all == slices and pair_count % 2 == 0 and spaces <= 2 * slices:
-        ops, width = op_count // spaces, 2 * nev
-        peers = max(spaces, slices)
-        every, gathered = pl.pallas_call(
-            functools.partial(exchange_kernel, spaces, slices),
-            out_shape=(
-                jax.ShapeDtypeStruct((op_count, nev, width), jnp.bfloat16),
-                jax.ShapeDtypeStruct((spaces, 2 * ops, width), jnp.float32),
-            ),
-            in_specs=[pl.BlockSpec(memory_space=pltpu.VMEM)] * 2,
-            out_specs=[pl.BlockSpec(memory_space=pltpu.VMEM)] * 2,
-            scratch_shapes=[
+                pltpu.VMEM((op_count, nev, width), jnp.float32),
                 pltpu.VMEM((spaces, ops, nev, width), jnp.float32),
                 pltpu.VMEM((spaces // 2, ops, nev, width), jnp.float32),
                 pltpu.VMEM((slices, ops, nev, width), jnp.bfloat16),
@@ -586,12 +580,39 @@
             compiler_params=pltpu.CompilerParams(
                 collective_id=0, has_side_effects=True, vmem_limit_bytes=VMEM_LIMIT
             ),
-            name="exchange",
-        )(partial_sums, both)
+            name="whole",
+        )(v, u, cos_all, sin_all, both)
         found = gathered[:, :, :t_all].reshape(spaces, 2, ops, t_all)
         correlator = jnp.swapaxes(found, 0, 1).reshape(2, op_count, 1, t_all)
         elementals = jnp.swapaxes(every.reshape(op_count, nev, 2, nev), 1, 2)[:, None]
         return (smeared.reshape(eigvecs.shape), elementals, correlator)
+
+    narrow = v.astype(jnp.bfloat16)
+    up = along(narrow, -1, 0)
+    down = up if z_total == 2 else along(narrow, 1, 0)
+    zlink = along(u[2], 1, 0)
+    edge = jnp.stack(
+        link_times(
+            lambda k: u[1, k : k + 1, sites - LX :], lambda i: v[i, :, sites - LX :], True
+        )
+    )
+    row_above = along(v[:, :, :LX], 0, -1)
+    row_below = along(edge, 0, 1)
+    smeared, partial_sums = pl.pallas_call(
+        functools.partial(smear_kernel, 1.0 / math.sqrt(3.0 * z_total * LX * LX)),
+        out_shape=(
+            jax.ShapeDtypeStruct((6, nev, sites), jnp.bfloat16),
+            jax.ShapeDtypeStruct((op_count, nev, 2 * nev), jnp.float32),
+        ),
+        scratch_shapes=[
+            pltpu.VMEM((6, nev, lanes), jnp.float32),
+            pltpu.VMEM((6, nev, sites), jnp.float32),
+            pltpu.VMEM((6, nev, lanes), jnp.float32),
+            pltpu.VMEM((6, nev, sites), jnp.float32),
+        ],
+        compiler_params=pltpu.CompilerParams(vmem_limit_bytes=VMEM_LIMIT),
+        name="smear",
+    )(v, up, down, u, zlink, row_above, row_below, cos_all, sin_all)
 
     if op_count % spaces == 0:
         own = lax.psum_scatter(partial_sums, "space", scatter_dimension=0, tiled=True)

time: 67.5 us -> 57.8 us (0.86)
  Pallas kernels: 57 us -> 48.9 us
  other arithmetic: 2.49 us -> 1.68 us
  local copies, waits for them, and re-layouts: 7.01 us -> 6.32 us
    pallas_call x2 -> x1, Pallas kernels: 57 us -> 48.9 us  [local(): pl.pallas_call(functools.partial(whole_kernel, spaces, slices, norm_scale...]
    unnamed x1, other arithmetic: 0.97 us -> 0.16 us
    unnamed x3 -> x7, local copies, waits for them, and re-layouts: 3.56 us -> 2.87 us
where the time goes in v4:
time: 57.8 us; the launch traced here: 57.6 us
  Pallas kernels  48.9 us (85%)
  local copies, waits for them, and re-layouts  6.32 us (11%)
  other arithmetic  1.68 us (3%)
  between operations  0.74 us (1%)
    pallas_call x1, Pallas kernels, local(): pl.pallas_call(functools.partial(whole_kernel, spaces, slices, norm_scale...  48.9 us
    unnamed x7, local copies, waits for them, and re-layouts  2.87 us
    reshape x2, local copies, waits for them, and re-layouts, local(): every.reshape(op_count, nev, 2, nev)  1.65 us

profile of v4, /device:TPU:0, one launch (start us, length us, event | category | flops | bytes accessed | tf_op | source)
XLA Modules:
  0.0 57.6 jit_solution(17791144120073642491)
XLA Ops:
  0.7 0.7 %fusion.17 = f32[32]{0:T(128)S(1)} fusion(s32[32,3]{0,1:T(4,128)} %param.7, s32[]{:T(128)S(6)} %select_n.51), kind=kLoop, calls=%fused_computation.34 | loop fusion | flops 448 | bytes 260 | tf_op jit(solution)/shard_map/add | solution.py:29
  1.4 0.8 %slice_bitcast_fusion.3 = (s32[32]{0:T(128)S(1)}, s32[32]{0:T(128)S(1)}) fusion(s32[32,3]{0,1:T(4,128)} %param.7), kind=kLoop, calls=%fused_computation.37 | loop fusion | bytes 512 | tf_op jit(solution)/shard_map/mul | solution.py:22
  2.1 0.2 sine_negate_fusion
  2.4 1.8 %copy.11 = bf16[1,4,2,4,4,64,64]{6,5,4,3,1,2,0:T(8,128)(2,1)S(1)} copy(bf16[1,4,2,4,4,64,64]{6,5,4,3,2,1,0:T(8,128)(2,1)} %param.6) | data formatting | bytes 2097152 | tf_op args[2]
  4.1 0.1 slice_bitcast_fusion.1
  4.3 0.0 copy-start
  4.3 0.0 copy-start.1
  4.3 0.6 %pad_maximum_fusion.bc = bf16[4,1024,128]{2,1,0:T(8,128)(2,1)S(1)} fusion(bf16[4,1024,64]{2,1,0:T(8,128)(2,1)S(1)} %get-tuple-element.16, bf16[4,1024,64]{2,1,0:T(8,128)(2,1)S(1)} %get-tuple-element.15), kind=kLoop, calls=%fused_computation.2 | loop fusion | flops 2097152 | bytes 2097152 | tf_op jit(solution)/shard_map/concatenate | solution.py:533
  4.9 0.4 copy-done
  5.3 0.0 copy-done.1
  5.3 0.2 reduce
  5.5 48.9 %whole.1 = (bf16[6,64,144]{2,1,0:T(8,128)(2,1)S(1)}, bf16[32,64,128]{2,1,0:T(8,128)(2,1)S(1)}, f32[8,8,128]{2,1,0:T(8,128)S(1)}) custom-call(f32[6,64,144]{2,1,0:T(8,128)S(1)} %bitcast.28, f32[3,18,144]{2,1,0:T(8,128)S(1)} %reshape.49.u, f32[32,144]{1,0:T(8,128)S(1)} %get-tuple-element.18.cs, f32[32,144]{1,0:T(8,128)S(1)} %get-tuple-element.17.sn, ...), custom_call_target="tpu_custom_call" | custom-call | tf_op jit(solution)/shard_map/whole/pallas_call | solution.py:548
  54.4 0.4 reshape.52
  54.8 1.2 %copy.19 = bf16[32,64,2,64]{3,1,2,0:T(8,128)(2,1)} copy(bf16[32,64,2,64]{3,2,1,0:T(2,128)(2,1)S(1)} %reshape.52) | data formatting | bytes 1048576 | tf_op jit(solution)/shard_map/reshape | solution.py:587
  56.1 0.2 copy.13
  56.3 0.7 %reshape.54 = f32[2,32,1,4]{1,3,0,2:T(4,128)} reshape(f32[2,8,4,4]{2,1,3,0:T(8,128)S(1)} %bitcast.33) | data formatting | bytes 2048 | tf_op jit(solution)/shard_map/reshape | solution.py:586
  56.9 0.7 %copy.21 = bf16[1,2,3,64,1,144]{5,3,4,2,1,0:T(8,128)(2,1)} copy(bf16[1,2,3,64,1,144]{5,3,4,2,1,0:T(8,128)(2,1)S(1)} %bitcast.29) | data formatting | bytes 221184
  (3 shorter events, 0.1 us)
Async XLA Ops:
  4.3 1.0 %copy-start = (f32[1,2,3,64,1,144]{5,4,3,2,1,0:T(1,128)S(1)}, f32[1,2,3,64,1,144]{5,4,3,2,1,0:T(1,128)}, u32[]{:S(2)}) copy-start(f32[1,2,3,64,1,144]{5,4,3,2,1,0:T(1,128)} %param.4) | copy-start | bytes 663556
  4.3 1.0 %copy-start.1 = (f32[3,1,2,3,3,1,144]{6,5,4,3,2,1,0:T(1,128)S(1)}, f32[3,1,2,3,3,1,144]{6,5,4,3,2,1,0:T(1,128)}, u32[]{:S(2)}) copy-start(f32[3,1,2,3,3,1,144]{6,5,4,3,2,1,0:T(1,128)} %param.5) | copy-start | bytes 93316

commit v5 on v4

--- a/solution.py
+++ b/solution.py
@@ -343,7 +343,7 @@
 
 
 def exchange(
-    form, spaces, slices, partial, bc, every, gathered, inbox, middle, far, left, b2, weights, tile, send, recv
+    form, spaces, slices, partial, blocks, every, gathered, inbox, middle, far, left, bc, b2, weights, tile, send, recv
 ):
     me, mine = lax.axis_index("space"), lax.axis_index("tm")
     ops, nev, width = inbox.shape[1:]
@@ -388,7 +388,10 @@
         form(there + side)
         if k > 0:
             hand_on(order[k - 1])
-    b2[...] = signed_roll_3d(bc)
+    for t in range(blocks.shape[0]):
+        re, im = blocks[t, 0], blocks[t, 1]
+        bc[t] = jnp.concatenate([re, im], axis=1)
+        b2[t] = jnp.concatenate([-im, re], axis=1)
     total = hand_on(0)
     for d in order[:-1]:
         along[d].wait_recv()
@@ -498,14 +501,6 @@
     fars = [far_copy(d) for d in range(1, slices)]
     for copy in list(beside.values()) + list(along.values()) + fars + shares + passes + ends:
         copy.wait_send()
-
-
-def signed_roll_3d(ref):
-    block = ref[...].astype(jnp.float32)
-    half = block.shape[-1] // 2
-    turned = pltpu.roll(block, half, 2)
-    low = lax.broadcasted_iota(jnp.int32, block.shape, 2) < half
-    return jnp.where(low, -turned, turned).astype(jnp.bfloat16)
 
 
 def local(eigvecs, gauge_links, perambulators, momenta):
@@ -572,6 +567,7 @@
                 pltpu.VMEM((slices, ops, nev, width), jnp.bfloat16),
                 pltpu.VMEM((pair_count * nev, ops * width), jnp.bfloat16),
                 pltpu.VMEM((t_all, pair_count * nev, width), jnp.bfloat16),
+                pltpu.VMEM((t_all, pair_count * nev, width), jnp.bfloat16),
                 pltpu.VMEM((ops * width, width), jnp.bfloat16),
                 pltpu.VMEM((2 * ops, width), jnp.float32),
                 pltpu.SemaphoreType.DMA((6, peers)),
@@ -581,7 +577,7 @@
                 collective_id=0, has_side_effects=True, vmem_limit_bytes=VMEM_LIMIT
             ),
             name="whole",
-        )(v, u, cos_all, sin_all, both)
+        )(v, u, cos_all, sin_all, blocks)
         found = gathered[:, :, :t_all].reshape(spaces, 2, ops, t_all)
         correlator = jnp.swapaxes(found, 0, 1).reshape(2, op_count, 1, t_all)
         elementals = jnp.swapaxes(every.reshape(op_count, nev, 2, nev), 1, 2)[:, None]

time: 57.8 us -> 58.1 us (level)
    unnamed x1, other arithmetic: 0.16 us -> 0.97 us
    unnamed x7 -> x4, local copies, waits for them, and re-layouts: 2.87 us -> 3.29 us
where the time goes in v5:
time: 58.1 us; the launch traced here: 57.8 us
  Pallas kernels  48.6 us (84%)
  local copies, waits for them, and re-layouts  6.61 us (11%)
  other arithmetic  1.91 us (3%)
  between operations  0.7 us (1%)
    pallas_call x1, Pallas kernels, local(): pl.pallas_call(functools.partial(whole_kernel, spaces, slices, norm_scale...  48.6 us
    unnamed x4, local copies, waits for them, and re-layouts  3.29 us
    reshape x2, local copies, waits for them, and re-layouts, local(): every.reshape(op_count, nev, 2, nev)  1.65 us

profile of v5, /device:TPU:0, one launch (start us, length us, event | category | flops | bytes accessed | tf_op | source)
XLA Modules:
  0.0 57.8 jit_solution(8022989661199822880)
XLA Ops:
  0.7 0.7 %fusion.17 = f32[32]{0:T(128)S(1)} fusion(s32[32,3]{0,1:T(4,128)} %param.7, s32[]{:T(128)S(6)} %select_n.51), kind=kLoop, calls=%fused_computation.31 | loop fusion | flops 448 | bytes 260 | tf_op jit(solution)/shard_map/add | solution.py:29
  1.3 0.8 %slice_bitcast_fusion.1 = (s32[32]{0:T(128)S(1)}, s32[32]{0:T(128)S(1)}) fusion(s32[32,3]{0,1:T(4,128)} %param.7), kind=kLoop, calls=%fused_computation.34 | loop fusion | bytes 512 | tf_op jit(solution)/shard_map/mul | solution.py:22
  2.1 0.2 sine_negate_fusion
  2.4 1.0 %reduce = f32[3,2,3,3,144]{4,3,2,1,0:T(4,128)S(1)} reduce(f32[3,1,2,3,3,1,144]{6,5,4,3,2,1,0:T(1,128)} %param.5, f32[]{:T(128)} %constant.84), dimensions={1,5}, to_apply=%param.5.reduce_sub_computation | reduce | bytes 62212 | tf_op args[1]
  3.4 1.0 %copy.14 = f32[1,2,3,64,1,144]{5,3,4,2,1,0:T(8,128)S(1)} copy(f32[1,2,3,64,1,144]{5,4,3,2,1,0:T(1,128)} %param.4) | data formatting | bytes 442368
  4.4 0.0 copy-start
  4.4 1.6 %copy-done = bf16[1,4,2,4,4,64,64]{6,5,4,3,2,1,0:T(8,128)(2,1)S(1)} copy-done((bf16[1,4,2,4,4,64,64]{6,5,4,3,2,1,0:T(8,128)(2,1)S(1)}, bf16[1,4,2,4,4,64,64]{6,5,4,3,2,1,0:T(8,128)(2,1)}, u32[]{:S(2)}) %copy-start) | copy-done | bytes 1048600
  6.0 48.6 %whole.1 = (bf16[6,64,144]{2,1,0:T(8,128)(2,1)S(1)}, bf16[32,64,128]{2,1,0:T(8,128)(2,1)S(1)}, f32[8,8,128]{2,1,0:T(8,128)S(1)}) custom-call(f32[6,64,144]{2,1,0:T(8,128)S(1)} %bitcast.25, f32[3,18,144]{2,1,0:T(8,128)S(1)} %reshape.49.u, f32[32,144]{1,0:T(8,128)S(1)} %get-tuple-element.16.cs, f32[32,144]{1,0:T(8,128)S(1)} %get-tuple-element.15.sn, ...), custom_call_target="tpu_custom_call" | custom-call | tf_op jit(solution)/shard_map/whole/pallas_call | solution.py:543
  54.6 0.2 copy.11
  54.8 0.7 %reshape.54 = f32[2,32,1,4]{1,3,0,2:T(4,128)} reshape(f32[2,8,4,4]{2,1,3,0:T(8,128)S(1)} %bitcast.29) | data formatting | bytes 2048 | tf_op jit(solution)/shard_map/reshape | solution.py:582
  55.5 0.4 reshape.52
  55.9 1.2 %copy.17 = bf16[32,64,2,64]{3,1,2,0:T(8,128)(2,1)} copy(bf16[32,64,2,64]{3,2,1,0:T(2,128)(2,1)S(1)} %reshape.52) | data formatting | bytes 1048576 | tf_op jit(solution)/shard_map/reshape | solution.py:583
  57.1 0.7 %copy.19 = bf16[1,2,3,64,1,144]{5,3,4,2,1,0:T(8,128)(2,1)} copy(bf16[1,2,3,64,1,144]{5,3,4,2,1,0:T(8,128)(2,1)S(1)} %bitcast.26) | data formatting | bytes 221184
  (2 shorter events, 0.0 us)
Async XLA Ops:
  4.4 1.6 %copy-start = (bf16[1,4,2,4,4,64,64]{6,5,4,3,2,1,0:T(8,128)(2,1)S(1)}, bf16[1,4,2,4,4,64,64]{6,5,4,3,2,1,0:T(8,128)(2,1)}, u32[]{:S(2)}) copy-start(bf16[1,4,2,4,4,64,64]{6,5,4,3,2,1,0:T(8,128)(2,1)} %param.6) | copy-start | bytes 3145732
